TPU v7x, 32 devices: a whole 2x2x4 slice. The times are simulated.
32 devices in a mesh: fsdp: 8 (over z, y), rep: 4 (over x, core).
Axes of the slice: x: 2, y: 2, z: 4, core: 2. Of those that a mesh axis runs over, the one named last changes fastest.
Arguments:
- tokens: bfloat16 [32768, 1024], P(('fsdp', 'rep')), may hold values from -6 to 6
- cotangent: bfloat16 [32768, 1024], P(('fsdp', 'rep')), may hold values from -6 to 6
- doc_ids: int32 [32768], P(('fsdp', 'rep')), may hold values from 0 to 7, as said below
- w_qkv: float32 [1024, 3072], P(('fsdp', 'rep')), may hold values from -0.1875 to 0.1875
- w_out: float32 [1024, 1024], P(('fsdp', 'rep')), may hold values from -0.75 to 0.75
- w_in: float32 [1024, 4096], P(('fsdp', 'rep')), may hold values from -0.1875 to 0.1875
- w_down: float32 [4096, 1024], P(('fsdp', 'rep')), may hold values from -0.09375 to 0.09375
- vectors: float32 [13312], P(('fsdp', 'rep'))
- first_qkv: float32 [1024, 3072], P(('fsdp', 'rep')), may hold values from -0.0002 to 0.0002
- first_out: float32 [1024, 1024], P(('fsdp', 'rep')), may hold values from -0.0002 to 0.0002
- first_in: float32 [1024, 4096], P(('fsdp', 'rep')), may hold values from -0.0002 to 0.0002
- first_down: float32 [4096, 1024], P(('fsdp', 'rep')), may hold values from -0.0002 to 0.0002
- first_vectors: float32 [13312], P(('fsdp', 'rep')), may hold values from -0.0002 to 0.0002
- second_qkv: float32 [1024, 3072], P(('fsdp', 'rep')), may hold values from 1e-09 to 1e-07
- second_out: float32 [1024, 1024], P(('fsdp', 'rep')), may hold values from 1e-09 to 1e-07
- second_in: float32 [1024, 4096], P(('fsdp', 'rep')), may hold values from 1e-10 to 1e-08
- second_down: float32 [4096, 1024], P(('fsdp', 'rep')), may hold values from 1e-09 to 1e-07
- second_vectors: float32 [13312], P(('fsdp', 'rep')), may hold values from 1e-09 to 1e-07
Outputs:
- output: bfloat16 [32768, 1024], P(('fsdp', 'rep'))
- input_grad: float32 [32768, 1024], P(('fsdp', 'rep'))
- grad_norm: float32 [1], replicated
- grad_qkv: float32 [1024, 3072], P(('fsdp', 'rep'))
- grad_out: float32 [1024, 1024], P(('fsdp', 'rep'))
- grad_in: float32 [1024, 4096], P(('fsdp', 'rep'))
- grad_down: float32 [4096, 1024], P(('fsdp', 'rep'))
- grad_vectors: float32 [13312], P(('fsdp', 'rep'))
- new_first_qkv: float32 [1024, 3072], P(('fsdp', 'rep'))
- new_first_out: float32 [1024, 1024], P(('fsdp', 'rep'))
- new_first_in: float32 [1024, 4096], P(('fsdp', 'rep'))
- new_first_down: float32 [4096, 1024], P(('fsdp', 'rep'))
- new_first_vectors: float32 [13312], P(('fsdp', 'rep'))
- new_second_qkv: float32 [1024, 3072], P(('fsdp', 'rep'))
- new_second_out: float32 [1024, 1024], P(('fsdp', 'rep'))
- new_second_in: float32 [1024, 4096], P(('fsdp', 'rep'))
- new_second_down: float32 [4096, 1024], P(('fsdp', 'rep'))
- new_second_vectors: float32 [13312], P(('fsdp', 'rep'))
- change_qkv: float32 [1024, 3072], P(('fsdp', 'rep'))
- change_out: float32 [1024, 1024], P(('fsdp', 'rep'))
- change_in: float32 [1024, 4096], P(('fsdp', 'rep'))
- change_down: float32 [4096, 1024], P(('fsdp', 'rep'))
- change_vectors: float32 [13312], P(('fsdp', 'rep'))
Inputs may be any that keep to these rules, and one draw needn't show every extreme that they name: Within each block of 1024 tokens (one device's rows) doc_ids starts at 0 and rises by 0 or 1 from token to token; some block holds 8 documents and some block a single document of 1024 tokens.
All inputs are finite; a program needn't handle non-finite values.
Results may differ from a plain program's by a relative error of at most 0.012.
The roundings to bfloat16 on the way count: a program that leaves them out, or rounds other values in their place, can miss the bound.
Values may be sent and summed in bfloat16 or wider, within the bound.
No kernel may reach another device: no remote copies, remote signals or barrier semaphores. Data moves between devices by JAX's collectives and lax.ppermute only.
A program may use at most 256 MiB of HBM per device.

v0:
```python
import math

import jax
import jax.numpy as jnp
from jax import lax
from jax.sharding import PartitionSpec as P

D = 1024
FF = 4096
HEAD_DIM = 64
ROT = 16
STEPS = 10


first_decay = 0.9
second_decay = 0.95
adam_eps = 1e-08
weight_decay = 0.1
learn_rate = 0.02
clip_limit = 1.0
norm_eps = 1e-05


def layer_norm(inputs, gain, shift):
    centre = inputs - jnp.mean(inputs, axis=-1, keepdims=True)
    spread = jnp.mean(centre * centre, axis=-1, keepdims=True)
    return centre * lax.rsqrt(spread + norm_eps) * gain + shift


def positions_of(segments):
    index = jnp.arange(segments.shape[0], dtype=jnp.int32)
    starts = jnp.concatenate([jnp.ones((1,), dtype=bool), segments[1:] != segments[:-1]])
    first = lax.cummax(jnp.where(starts, index, jnp.zeros_like(index)), axis=0)
    return index - first


def rotary_tables(positions):
    half = ROT // 2
    freqs = jnp.exp(jnp.arange(half, dtype=jnp.float32) * (-2.0 * math.log(10000.0) / ROT))
    angles = positions.astype(jnp.float32)[:, None] * freqs[None, :]
    return (jnp.cos(angles)[:, None, :], jnp.sin(angles)[:, None, :])


def rotate_part(heads_in, cosine, sine):
    half = ROT // 2
    lower = heads_in[..., :half]
    upper = heads_in[..., half:ROT]
    return jnp.concatenate(
        [lower * cosine - upper * sine, upper * cosine + lower * sine, heads_in[..., ROT:]], axis=-1
    )


def unrotate_part(grads, cosine, sine):
    half = ROT // 2
    lower = grads[..., :half]
    upper = grads[..., half:ROT]
    return jnp.concatenate(
        [lower * cosine + upper * sine, upper * cosine - lower * sine, grads[..., ROT:]], axis=-1
    )


def split_vector(vector):
    cuts = [3 * D, 4 * D, 4 * D + FF, 5 * D + FF, 6 * D + FF, 7 * D + FF, 8 * D + FF]
    return jnp.split(vector, cuts)


def gelu_exact(values):
    return jax.nn.gelu(values, approximate=False)


def adam_step(weight, grad, first, second, clip, count):
    scaled = grad * clip
    new_first = first_decay * first + (1.0 - first_decay) * scaled
    new_second = second_decay * second + (1.0 - second_decay) * scaled * scaled
    fix_one = 1.0 - first_decay**count
    fix_two = 1.0 - second_decay**count
    change = -learn_rate * (
        new_first / fix_one / (jnp.sqrt(new_second / fix_two) + adam_eps) + weight_decay * weight
    )
    return (new_first, new_second, change)


def per_device(
    tokens,
    cotangent,
    doc_ids,
    w_qkv,
    w_out,
    w_in,
    w_down,
    vectors,
    first_qkv,
    first_out,
    first_in,
    first_down,
    first_vectors,
    second_qkv,
    second_out,
    second_in,
    second_down,
    second_vectors,
):
    qkv_matrix, out_matrix, in_matrix, down_matrix, vector_all = (
        lax.all_gather(w_qkv.astype(jnp.bfloat16), ("fsdp", "rep"), axis=0, tiled=True),
        lax.all_gather(w_out.astype(jnp.bfloat16), ("fsdp", "rep"), axis=0, tiled=True),
        lax.all_gather(w_in.astype(jnp.bfloat16), ("fsdp", "rep"), axis=0, tiled=True),
        lax.all_gather(w_down.astype(jnp.bfloat16), ("fsdp", "rep"), axis=0, tiled=True),
        lax.all_gather(vectors.astype(jnp.bfloat16), ("fsdp", "rep"), axis=0, tiled=True),
    )
    length = tokens.shape[0]
    heads = D // HEAD_DIM
    scale = HEAD_DIM ** (-0.5)
    b_qkv, b_out, b_in, b_down, gain_one, shift_one, gain_two, shift_two = split_vector(
        vector_all.astype(jnp.float32)
    )
    inputs = tokens.astype(jnp.float32)
    cosine, sine = rotary_tables(positions_of(doc_ids))
    index = jnp.arange(length, dtype=jnp.int32)
    allowed = (doc_ids[:, None] == doc_ids[None, :]) & (index[:, None] >= index[None, :])
    normed_a = layer_norm(inputs, gain_one, shift_one).astype(jnp.bfloat16)
    normed_m = layer_norm(inputs, gain_two, shift_two).astype(jnp.bfloat16)
    joined = (jnp.dot(normed_a, qkv_matrix, preferred_element_type=jnp.float32) + b_qkv).reshape(
        length, 3, heads, HEAD_DIM
    )
    query_heads = rotate_part(joined[:, 0], cosine, sine).astype(jnp.bfloat16).transpose(1, 0, 2)
    key_heads = rotate_part(joined[:, 1], cosine, sine).astype(jnp.bfloat16).transpose(1, 0, 2)
    value_heads = joined[:, 2].astype(jnp.bfloat16).transpose(1, 0, 2)

    def head_forward(parts):
        query, key_part, value = parts
        scores = jnp.dot(query, key_part.T, preferred_element_type=jnp.float32) * scale
        scores = jnp.where(allowed, scores, -1e30)
        peak = jnp.max(scores, axis=-1, keepdims=True)
        weights = jnp.exp(scores - peak)
        total = jnp.sum(weights, axis=-1, keepdims=True)
        probs = weights / total
        mixed_head = jnp.dot(probs.astype(jnp.bfloat16), value, preferred_element_type=jnp.float32)
        return (mixed_head, (peak + jnp.log(total))[:, 0])

    mixed, logsum = lax.map(head_forward, (query_heads, key_heads, value_heads))
    merged = mixed.transpose(1, 0, 2).reshape(length, D).astype(jnp.bfloat16)
    attended = jnp.dot(merged, out_matrix, preferred_element_type=jnp.float32) + b_out
    hidden = jnp.dot(normed_m, in_matrix, preferred_element_type=jnp.float32) + b_in
    active = gelu_exact(hidden).astype(jnp.bfloat16)
    fed = jnp.dot(active, down_matrix, preferred_element_type=jnp.float32) + b_down
    output = (inputs + attended + fed).astype(jnp.bfloat16)
    back_qkv, back_out, back_in, back_down = (
        lax.all_gather(w_qkv.astype(jnp.bfloat16), ("fsdp", "rep"), axis=0, tiled=True),
        lax.all_gather(w_out.astype(jnp.bfloat16), ("fsdp", "rep"), axis=0, tiled=True),
        lax.all_gather(w_in.astype(jnp.bfloat16), ("fsdp", "rep"), axis=0, tiled=True),
        lax.all_gather(w_down.astype(jnp.bfloat16), ("fsdp", "rep"), axis=0, tiled=True),
    )
    grad_float = cotangent.astype(jnp.float32)
    grad_down_w = jnp.dot(active.T, cotangent, preferred_element_type=jnp.float32)
    grad_out_w = jnp.dot(merged.T, cotangent, preferred_element_type=jnp.float32)
    grad_active = jnp.dot(cotangent, back_down.T, preferred_element_type=jnp.float32)
    gelu_pull = jax.vjp(gelu_exact, hidden)[1]
    grad_hidden = gelu_pull(grad_active)[0].astype(jnp.bfloat16)
    grad_in_w = jnp.dot(normed_m.T, grad_hidden, preferred_element_type=jnp.float32)
    grad_normed_m = jnp.dot(grad_hidden, back_in.T, preferred_element_type=jnp.float32)
    grad_merged = jnp.dot(cotangent, back_out.T, preferred_element_type=jnp.float32).astype(
        jnp.bfloat16
    )
    grad_heads = grad_merged.reshape(length, heads, HEAD_DIM).transpose(1, 0, 2)

    def head_backward(parts):
        query, key_part, value, grad_head, logsum_head = parts
        scores = jnp.dot(query, key_part.T, preferred_element_type=jnp.float32) * scale
        probs = jnp.where(allowed, jnp.exp(scores - logsum_head[:, None]), 0.0)
        grad_value = jnp.dot(
            probs.astype(jnp.bfloat16).T, grad_head, preferred_element_type=jnp.float32
        )
        grad_probs = jnp.dot(grad_head, value.T, preferred_element_type=jnp.float32)
        inner = jnp.sum(grad_probs * probs, axis=-1, keepdims=True)
        grad_scores = (probs * (grad_probs - inner)).astype(jnp.bfloat16)
        grad_query = jnp.dot(grad_scores, key_part, preferred_element_type=jnp.float32) * scale
        grad_key = jnp.dot(grad_scores.T, query, preferred_element_type=jnp.float32) * scale
        return (grad_query, grad_key, grad_value)

    grad_query, grad_key, grad_value = lax.map(
        head_backward, (query_heads, key_heads, value_heads, grad_heads, logsum)
    )
    grad_joined = (
        jnp.stack(
            [
                unrotate_part(grad_query.transpose(1, 0, 2), cosine, sine),
                unrotate_part(grad_key.transpose(1, 0, 2), cosine, sine),
                grad_value.transpose(1, 0, 2),
            ],
            axis=1,
        )
        .reshape(length, 3 * D)
        .astype(jnp.bfloat16)
    )
    grad_qkv_w = jnp.dot(normed_a.T, grad_joined, preferred_element_type=jnp.float32)
    grad_normed_a = jnp.dot(grad_joined, back_qkv.T, preferred_element_type=jnp.float32)
    norm_pull_a = jax.vjp(layer_norm, inputs, gain_one, shift_one)[1]
    grad_x_a, grad_gain_one, grad_shift_one = norm_pull_a(grad_normed_a)
    norm_pull_m = jax.vjp(layer_norm, inputs, gain_two, shift_two)[1]
    grad_x_m, grad_gain_two, grad_shift_two = norm_pull_m(grad_normed_m)
    input_grad = grad_float + grad_x_a + grad_x_m
    column_float = jnp.sum(grad_float, axis=0)
    grad_vector_all = jnp.concatenate(
        [
            jnp.sum(grad_joined.astype(jnp.float32), axis=0),
            column_float,
            jnp.sum(grad_hidden.astype(jnp.float32), axis=0),
            column_float,
            grad_gain_one,
            grad_shift_one,
            grad_gain_two,
            grad_shift_two,
        ]
    )
    shards = (
        lax.psum_scatter(grad_qkv_w, ("fsdp", "rep"), scatter_dimension=0, tiled=True),
        lax.psum_scatter(grad_out_w, ("fsdp", "rep"), scatter_dimension=0, tiled=True),
        lax.psum_scatter(grad_in_w, ("fsdp", "rep"), scatter_dimension=0, tiled=True),
        lax.psum_scatter(grad_down_w, ("fsdp", "rep"), scatter_dimension=0, tiled=True),
        lax.psum_scatter(grad_vector_all, ("fsdp", "rep"), scatter_dimension=0, tiled=True),
    )
    local_square = sum((jnp.sum(piece * piece) for piece in shards))
    total_square = lax.psum(local_square, ("fsdp", "rep"))
    norm = jnp.sqrt(total_square)
    clip = jnp.minimum(1.0, clip_limit / (norm + 1e-06))
    count = float(STEPS)
    masters = (w_qkv, w_out, w_in, w_down, vectors)
    firsts = (first_qkv, first_out, first_in, first_down, first_vectors)
    seconds = (second_qkv, second_out, second_in, second_down, second_vectors)
    results = [
        adam_step(w, g, f, s, clip, count) for w, g, f, s in zip(masters, shards, firsts, seconds)
    ]
    return (
        output,
        input_grad,
        norm.reshape(1),
        shards[0],
        shards[1],
        shards[2],
        shards[3],
        shards[4],
        results[0][0],
        results[1][0],
        results[2][0],
        results[3][0],
        results[4][0],
        results[0][1],
        results[1][1],
        results[2][1],
        results[3][1],
        results[4][1],
        results[0][2],
        results[1][2],
        results[2][2],
        results[3][2],
        results[4][2],
    )


def solution(mesh):
    in_specs = (
        P(("fsdp", "rep"), None),
        P(("fsdp", "rep"), None),
        P(("fsdp", "rep")),
        P(("fsdp", "rep"), None),
        P(("fsdp", "rep"), None),
        P(("fsdp", "rep"), None),
        P(("fsdp", "rep"), None),
        P(("fsdp", "rep")),
        P(("fsdp", "rep"), None),
        P(("fsdp", "rep"), None),
        P(("fsdp", "rep"), None),
        P(("fsdp", "rep"), None),
        P(("fsdp", "rep")),
        P(("fsdp", "rep"), None),
        P(("fsdp", "rep"), None),
        P(("fsdp", "rep"), None),
        P(("fsdp", "rep"), None),
        P(("fsdp", "rep")),
    )
    out_specs = (
        P(("fsdp", "rep"), None),
        P(("fsdp", "rep"), None),
        P(),
        P(("fsdp", "rep"), None),
        P(("fsdp", "rep"), None),
        P(("fsdp", "rep"), None),
        P(("fsdp", "rep"), None),
        P(("fsdp", "rep")),
        P(("fsdp", "rep"), None),
        P(("fsdp", "rep"), None),
        P(("fsdp", "rep"), None),
        P(("fsdp", "rep"), None),
        P(("fsdp", "rep")),
        P(("fsdp", "rep"), None),
        P(("fsdp", "rep"), None),
        P(("fsdp", "rep"), None),
        P(("fsdp", "rep"), None),
        P(("fsdp", "rep")),
        P(("fsdp", "rep"), None),
        P(("fsdp", "rep"), None),
        P(("fsdp", "rep"), None),
        P(("fsdp", "rep"), None),
        P(("fsdp", "rep")),
    )
    return jax.shard_map(
        per_device, mesh=mesh, in_specs=in_specs, out_specs=out_specs, check_vma=False
    )
```

profile of v0, /device:TPU:0, one launch (start us, length us, event | category | flops | bytes accessed | tf_op | source)
XLA Modules:
  0.0 1157.1 jit_solution(12558561993541881553)
XLA Ops:
  15.4 42.3 %all-reduce = bf16[13312]{0:T(1024)(128)(2,1)S(1)} all-reduce(bf16[13312]{0:T(1024)(128)(2,1)S(1)} %dynamic-update-slice), channel_id=1, replica_groups=mesh['fsdp'=8,'rep'=4] {'fsdp','rep'}, use_global_device_ids=true, to_apply=%add | all-reduce | flops 13312 | bytes 53248
  65.8 4.8 all-gather.7.cloned.1.call-done
  70.6 5.9 convolution_convert_fusion
  81.3 61.2 %all-gather.5.cloned.1.call-done = bf16[1024,3072]{1,0:T(8,128)(2,1)} async-done(((bf16[32,3072]{1,0:T(8,128)(2,1)}), bf16[1024,3072]{1,0:T(8,128)(2,1)}) %all-gather.5.cloned.1.call-update) | async-done | bytes 6291472 | tf_op jit(solution)/shard_map/all_gather | solution.py:104
  142.4 12.7 %broadcast_add_fusion = f32[1024,3072]{1,0:T(8,128)} fusion(f32[3072]{0:T(1024)S(1)} %split.34, bf16[1024,3072]{1,0:T(8,128)(2,1)} %all-gather.5.cloned.1.call-done, bf16[1024,1024]{1,0:T(8,128)(2,1)S(1)} %copy-done.1, f32[1024]{0:T(1024)S(1)} %get-tuple-element.306, f32[1024]{0:T(1024)S(1)} %get-tuple-element.305, f32[1024]{0:T(1024)S(1)} %fusion.84, ...), kind=kOutput, calls=%fused_computation.78 | convolution fusion | flops 6451888128 | bytes 21000192 | tf_op jit(solution)/shard_map/dot_general | solution.py:122
  155.1 12.6 %copy.57 = f32[1024,3072]{0,1:T(8,128)} copy(f32[1024,3072]{1,0:T(8,128)} %broadcast_add_fusion) | data formatting | bytes 25165824 | tf_op jit(solution)/shard_map/add | solution.py:122
  183.6 4.8 copy.59
  193.3 135.8 %while.30 = (s32[]{:T(128)}, bf16[16,1024,64]{1,2,0:T(8,128)(2,1)}, f32[16,1024]{1,0:T(8,128)S(1)}, bf16[16,1024,64]{2,1,0:T(8,128)(2,1)}, bf16[16,1024,64]{2,1,...) while((s32[]{:T(128)}, bf16[16,1024,64]{1,2,0:T(8,128)(2,1)}, ...), condition=%wide.region_7.8_spmd.clone.clone, body=%wide.region_4.0_spmd.clone.sunk.clone | while | flops 279968768 | bytes 30460012 | solution.py:140
  329.0 6.5 fusion.108
  335.6 192.2 %while.31 = (s32[]{:T(128)}, f32[16,1024,64]{1,2,0:T(8,128)}, f32[16,1024,64]{1,2,0:T(8,128)}, bf16[16,1024,64]{1,2,0:T(8,128)(2,1)}, bf16[16,1024,64]{2,1,0:T(8...) while((s32[]{:T(128)}, f32[16,1024,64]{1,2,0:T(8,128)}, ...), condition=%wide.region_10.11_spmd.clone.clone, body=%wide.region_8.10_spmd.clone.sunk.clone | while | flops 683801600 | bytes 34112616 | solution.py:180
  540.7 10.1 fusion.90
  551.5 15.1 %fusion.88 = f32[1024,4096]{1,0:T(8,128)} fusion(bf16[1024,4096]{1,0:T(8,128)(2,1)} %all-gather.9.cloned.1.call-done, bf16[1024,1024]{1,0:T(8,128)(2,1)S(1)} %copy-done.1, f32[1024]{0:T(1024)S(1)} %copy-done.34, f32[1024]{0:T(1024)S(1)} %copy-done.21, f32[1024]{0:T(1024)S(1)} %fusion.84, f32[1024]{0:T(1024)S(1)} %broadcast_multiply_fusion), kind=kOutput, calls=%fused_computation.176 | convolution fusion | flops 8596226048 | bytes 27279360 | tf_op jit(solution)/shard_map/dot_general | solution.py:143
  566.6 51.9 %convert_reduce_fusion = (f32[4096]{0:T(1024)S(1)}, bf16[1024,4096]{1,0:T(8,128)(2,1)S(1)}, f32[1024,4096]{1,0:T(8,128)}) fusion(f32[1024,4096]{1,0:T(8,128)} %fusion.88, f32[4096]{0:T(1024)S(1)} %copy-done.20, bf16[1024,1024]{1,0:T(8,128)(2,1)} %param.23, bf16[4096,1024]{1,0:T(8,128)(2,1)} %all-gather.11.cloned.1.call-done), kind=kOutput, calls=%fused_computation.58 | convolution fusion | flops 8904503296 | bytes 52461568 | tf_op jit(solution)/shard_map/dot_general | solution.py:156
  621.8 12.2 %fusion.86 = f32[1024,4096]{1,0:T(8,128)} fusion(bf16[1024,4096]{1,0:T(8,128)(2,1)S(1)} %get-tuple-element.273, bf16[1024,1024]{1,0:T(8,128)(2,1)S(1)} %copy-done.2, f32[1024]{0:T(1024)S(1)} %copy-done.35, f32[1024]{0:T(1024)S(1)} %copy-done.22, f32[1024]{0:T(1024)S(1)} %copy-done.26, f32[1024]{0:T(1024)S(1)} %copy-done.19), kind=kOutput, calls=%fused_computation.175 | convolution fusion | flops 8596226048 | bytes 27279360 | tf_op jit(solution)/shard_map/dot_general | solution.py:159
  634.1 13.5 %multiply_convert_fusion.1 = bf16[1024,4096]{1,0:T(8,128)(2,1)S(1)} fusion(f32[1024,4096]{1,0:T(8,128)} %get-tuple-element.274, f32[1024,4096]{1,0:T(8,128)} %fusion.88, f32[4096]{0:T(1024)S(1)} %copy-done.20), kind=kLoop, calls=%fused_computation.60 | loop fusion | flops 16777216 | bytes 41959424 | tf_op jit(solution)/shard_map/convert_element_type | solution.py:144
  650.8 11.7 %fusion.109 = f32[4096,1024]{1,0:T(8,128)} fusion(bf16[1024,4096]{1,0:T(8,128)(2,1)S(1)} %multiply_convert_fusion.1, bf16[1024,1024]{1,0:T(8,128)(2,1)S(1)} %copy-done.5), kind=kOutput, calls=%fused_computation.188 | convolution fusion | flops 8589934592 | bytes 27262976 | tf_op jit(solution)/shard_map/dot_general | solution.py:154
  663.3 6.7 fusion.106
  670.0 12.9 %fusion.107 = f32[1024,1024]{1,0:T(8,128)S(1)} fusion(bf16[1024,4096]{1,0:T(8,128)(2,1)} %copy-done.38, bf16[1024,4096]{1,0:T(8,128)(2,1)} %all-gather.9.cloned.1.call-done), kind=kOutput, calls=%fused_computation.186 | convolution fusion | flops 8589934592 | bytes 20971520 | tf_op jit(solution)/shard_map/dot_general | solution.py:160
  682.9 10.9 fusion.96
  702.4 43.4 %all-reduce.1 = f32[13312]{0:T(1024)S(1)} all-reduce(f32[13312]{0:T(1024)S(1)} %constant_dynamic-update-slice_fusion), channel_id=6, replica_groups=mesh['fsdp'=8,'rep'=4] {'fsdp','rep'}, use_global_device_ids=true, to_apply=%region_30.31.clone | all-reduce | flops 13312 | bytes 106496
  751.0 140.5 %reduce-scatter.9.cloned.1.call-done = f32[32,4096]{1,0:T(8,128)} async-done(((f32[1024,4096]{1,0:T(8,128)}), f32[32,4096]{1,0:T(8,128)}) %reduce-scatter.9.cloned.1.call-update) | async-done | bytes 524304 | tf_op jit(solution)/shard_map/reduce_scatter | solution.py:218
  894.0 184.9 %reduce-scatter.11.cloned.1.call-done = f32[128,1024]{1,0:T(8,128)} async-done(((f32[4096,1024]{1,0:T(8,128)}), f32[128,1024]{1,0:T(8,128)}) %reduce-scatter.11.cloned.1.call-update) | async-done | bytes 524304 | tf_op jit(solution)/shard_map/reduce_scatter | solution.py:219
  1082.0 15.5 %fusion.77 = bf16[1024,1024]{1,0:T(8,128)(2,1)} fusion(bf16[1024,1024]{1,0:T(8,128)(2,1)S(1)} %copy-done.2, f32[1024,1024]{1,0:T(8,128)} %fusion.106, f32[1024]{0:T(1024)S(1)} %copy-done.33, f32[1024]{0:T(1024)S(1)} %copy-done.32, bf16[1024,4096]{1,0:T(8,128)(2,1)} %copy-done.3, bf16[4096,1024]{1,0:T(8,128)(2,1)} %all-gather.11.cloned.1.call-done), kind=kOutput, calls=%fused_computation.105 | convolution fusion | flops 8596226048 | bytes 25174016 | tf_op jit(solution)/shard_map/dot_general | solution.py:145
  1097.6 42.4 %psum.7 = f32[]{:T(128)} all-reduce(f32[]{:T(128)S(6)} %add.235), channel_id=1, replica_groups=mesh['fsdp'=8,'rep'=4] {'fsdp','rep'}, use_global_device_ids=true, to_apply=%region_32.33 | all-reduce | flops 1 | bytes 8 | tf_op jit(solution)/shard_map/psum | solution.py:223
  (392 shorter events, 413.6 us)
Async XLA Ops:
  7.2 63.4 %all-gather.7.cloned.1.call-start = ((), (), s32[]{:S(2)}) async-start(), calls=%async_computation.5 | async-start | bytes 2162688 | tf_op jit(solution)/shard_map/all_gather | solution.py:105
  9.0 133.5 %all-gather.5.cloned.1.call-start = ((), (), s32[]{:S(2)}) async-start(), calls=%async_computation.4 | async-start | bytes 6488064 | tf_op jit(solution)/shard_map/all_gather | solution.py:104
  10.7 540.1 %all-gather.9.cloned.1.call-start = ((), (), s32[]{:S(2)}) async-start(), calls=%async_computation.6 | async-start | bytes 8650752 | tf_op jit(solution)/shard_map/all_gather | solution.py:106
  12.6 554.0 %all-gather.11.cloned.1.call-start = ((), (), s32[]{:S(2)}) async-start(), calls=%async_computation.7 | async-start | bytes 8650752 | tf_op jit(solution)/shard_map/all_gather | solution.py:107
  14.4 732.0 %reduce-scatter.7.cloned.1.call-start = ((), (), s32[]{:S(2)}) async-start(), calls=%async_computation.9 | async-start | bytes 4325376 | tf_op jit(solution)/shard_map/reduce_scatter | solution.py:217
  58.3 479.7 %copy-start.23 = (f32[1024]{0:T(1024)}, f32[1024]{0:T(1024)S(1)}, u32[]{:S(2)}) copy-start(f32[1024]{0:T(1024)S(1)} %get-tuple-element.305) | copy-start | bytes 12292
  60.9 490.0 %copy-start.18 = (f32[1024]{0:T(1024)}, f32[1024]{0:T(1024)S(1)}, u32[]{:S(2)}) copy-start(f32[1024]{0:T(1024)S(1)} %broadcast_multiply_fusion) | copy-start | bytes 12292
  61.6 489.2 %copy-start.25 = (f32[1024]{0:T(1024)}, f32[1024]{0:T(1024)S(1)}, u32[]{:S(2)}) copy-start(f32[1024]{0:T(1024)S(1)} %fusion.84) | copy-start | bytes 12292
  335.5 412.5 %reduce-scatter.5.cloned.1.call-start = ((), (), s32[]{:S(2)}) async-start(), calls=%async_computation.8 | async-start | bytes 12976128 | tf_op jit(solution)/shard_map/reduce_scatter | solution.py:216
  550.8 340.8 %reduce-scatter.9.cloned.1.call-start = ((), (), s32[]{:S(2)}) async-start(), calls=%async_computation.10 | async-start | bytes 17301504 | tf_op jit(solution)/shard_map/reduce_scatter | solution.py:218
  566.6 55.2 %copy-start.2 = (bf16[1024,1024]{1,0:T(8,128)(2,1)S(1)}, bf16[1024,1024]{1,0:T(8,128)(2,1)}, u32[]{:S(2)}) copy-start(bf16[1024,1024]{1,0:T(8,128)(2,1)} %param.22) | copy-start | bytes 6291460
  566.6 55.2 %copy-start.19 = (f32[1024]{0:T(1024)S(1)}, f32[1024]{0:T(1024)}, u32[]{:S(2)}) copy-start(f32[1024]{0:T(1024)} %copy-done.18) | copy-start | bytes 12292
  566.6 55.2 %copy-start.22 = (f32[1024]{0:T(1024)S(1)}, f32[1024]{0:T(1024)}, u32[]{:S(2)}) copy-start(f32[1024]{0:T(1024)} %get-tuple-element.301) | copy-start | bytes 12292
  566.6 55.2 %copy-start.26 = (f32[1024]{0:T(1024)S(1)}, f32[1024]{0:T(1024)}, u32[]{:S(2)}) copy-start(f32[1024]{0:T(1024)} %copy-done.25) | copy-start | bytes 12292
  566.6 55.2 %copy-start.35 = (f32[1024]{0:T(1024)S(1)}, f32[1024]{0:T(1024)}, u32[]{:S(2)}) copy-start(f32[1024]{0:T(1024)} %get-tuple-element.302) | copy-start | bytes 12292
  634.0 444.8 %reduce-scatter.11.cloned.1.call-start = ((), (), s32[]{:S(2)}) async-start(), calls=%async_computation.11 | async-start | bytes 17301504 | tf_op jit(solution)/shard_map/reduce_scatter | solution.py:219
  697.9 384.0 %copy-start.32 = (f32[1024]{0:T(1024)S(1)}, f32[1024]{0:T(1024)}, u32[]{:S(2)}) copy-start(f32[1024]{0:T(1024)} %get-tuple-element.303) | copy-start | bytes 12292
  697.9 384.0 %copy-start.33 = (f32[1024]{0:T(1024)S(1)}, f32[1024]{0:T(1024)}, u32[]{:S(2)}) copy-start(f32[1024]{0:T(1024)} %get-tuple-element.304) | copy-start | bytes 12292
  746.5 394.2 %copy-start.31 = (f32[416]{0:T(512)}, f32[416]{0:T(512)S(1)}, u32[]{:S(2)}) copy-start(f32[416]{0:T(512)S(1)} %get-tuple-element.271) | copy-start | bytes 4996
  1082.0 58.8 %copy-start.30 = (f32[416]{0:T(512)S(1)}, f32[416]{0:T(512)}, u32[]{:S(2)}) copy-start(f32[416]{0:T(512)} %param.29) | copy-start | bytes 4996
  1082.0 58.8 %copy-start.36 = (f32[416]{0:T(512)S(1)}, f32[416]{0:T(512)}, u32[]{:S(2)}) copy-start(f32[416]{0:T(512)} %param.39) | copy-start | bytes 4996
  1082.0 58.8 %copy-start.37 = (f32[416]{0:T(512)S(1)}, f32[416]{0:T(512)}, u32[]{:S(2)}) copy-start(f32[416]{0:T(512)} %param.34) | copy-start | bytes 4996
  1082.0 59.4 %copy-start.7 = (f32[128,1024]{1,0:T(8,128)S(1)}, f32[128,1024]{1,0:T(8,128)}, u32[]{:S(2)}) copy-start(f32[128,1024]{1,0:T(8,128)} %param.28) | copy-start | bytes 1572868
  1082.0 62.1 %copy-start.8 = (f32[32,4096]{1,0:T(8,128)S(1)}, f32[32,4096]{1,0:T(8,128)}, u32[]{:S(2)}) copy-start(f32[32,4096]{1,0:T(8,128)} %param.27) | copy-start | bytes 1572868
  (40 other events, 651.4 us)
Sparse Core Ops, SparseCore 0:
  11.5 59.0 all-gather.6
  74.0 68.3 all-gather.4
  145.9 75.9 all-gather.8
  225.2 76.0 all-gather.10
  335.7 140.3 reduce-scatter.6
  550.9 154.8 reduce-scatter.4
  708.8 182.7 reduce-scatter.8
  894.5 184.2 reduce-scatter.10
where the time goes:
time: 1170 us; the launch traced here: 1160 us
  matrix products  438 us (37%)
  waiting for transfers between devices  392 us (34%)
  blocking collectives  128 us (11%)
  local copies, waits for them, and re-layouts  92.6 us (8%)
  other arithmetic  85.2 us (7%)
  between operations  20.1 us (2%)
    reduce_scatter x1, waiting for transfers between devices, per_device(): lax.psum_scatter(grad_down_w, ('fsdp', 'rep'), scatter_dimension=0, tiled...  185 us
    reduce_scatter x1, waiting for transfers between devices, per_device(): lax.psum_scatter(grad_in_w, ('fsdp', 'rep'), scatter_dimension=0, tiled=T...  141 us
    unnamed x2, blocking collectives  85.7 us
    all_gather x1, waiting for transfers between devices, per_device(): lax.all_gather(w_qkv.astype(jnp.bfloat16), ('fsdp', 'rep'), axis=0, tiled...  61.2 us
    dot_general x16, matrix products, head_forward(): jnp.dot(probs.astype(jnp.bfloat16), value, preferred_element_type=jnp.flo...  60.4 us
    dot_general x1, matrix products, per_device(): jnp.dot(cotangent, back_down.T, preferred_element_type=jnp.float32)  51.9 us
    psum x1, blocking collectives, per_device(): total_square = lax.psum(local_square, ('fsdp', 'rep'))  42.4 us
    dot_general x16, matrix products, head_backward(): jnp.dot(grad_scores.T, query, preferred_element_type=jnp.float32) * scale  38.9 us
  transfers between devices with their start and end apart: 8, of which 4 were waited for; matrix products, arithmetic and copies ran while one was open for 47% of the time, Pallas kernels for 0%

commit v1 on v0

v1 whole, which is shorter than its diff:
```python
import functools
import math

import jax
import jax.numpy as jnp
from jax import lax
from jax.experimental import pallas as pl
from jax.experimental.pallas import tpu as pltpu
from jax.sharding import Mesh
from jax.sharding import PartitionSpec as P

D = 1024
FF = 4096
HEAD_DIM = 64
ROT = 16
STEPS = 10

first_decay = 0.9
second_decay = 0.95
adam_eps = 1e-08
weight_decay = 0.1
learn_rate = 0.02
clip_limit = 1.0
norm_eps = 1e-05

bf16 = jnp.bfloat16
f32 = jnp.float32

HEADS_STEP = 4
WIDTH = HEADS_STEP * HEAD_DIM
QUERY_ROWS = 256
FF_TILE = 512
TOKEN_TILE = 256
HALF = D // 2
VMEM_BYTES = 58 * 2**20


def mul(a, b, dim_a, dim_b):
    return lax.dot_general(a, b, (((dim_a,), (dim_b,)), ((), ())), preferred_element_type=f32)


def positions_of(segments):
    index = jnp.arange(segments.shape[0], dtype=jnp.int32)
    starts = jnp.concatenate([jnp.ones((1,), dtype=bool), segments[1:] != segments[:-1]])
    first = lax.cummax(jnp.where(starts, index, jnp.zeros_like(index)), axis=0)
    return index - first


def split_vector(vector):
    cuts = [3 * D, 4 * D, 4 * D + FF, 5 * D + FF, 6 * D + FF, 7 * D + FF, 8 * D + FF]
    return jnp.split(vector, cuts)


def adam_step(weight, grad, first, second, clip, count):
    scaled = grad * clip
    new_first = first_decay * first + (1.0 - first_decay) * scaled
    new_second = second_decay * second + (1.0 - second_decay) * scaled * scaled
    fix_one = 1.0 - first_decay**count
    fix_two = 1.0 - second_decay**count
    change = -learn_rate * (
        new_first / fix_one / (jnp.sqrt(new_second / fix_two) + adam_eps) + weight_decay * weight
    )
    return (new_first, new_second, change)


def call(kernel, grid, in_specs, out_specs, out_shape, args, after=(), scratch=(), aliases=None, flops=0, moved=0):
    count = len(args)

    def run(*refs):
        kernel(*refs[: 1 + count], *refs[1 + count + len(after) :])

    return pl.pallas_call(
        run,
        grid_spec=pltpu.PrefetchScalarGridSpec(
            num_scalar_prefetch=1,
            grid=grid,
            in_specs=list(in_specs) + [pl.BlockSpec(memory_space=pl.ANY)] * len(after),
            out_specs=list(out_specs),
            scratch_shapes=list(scratch),
        ),
        out_shape=list(out_shape),
        input_output_aliases=aliases or {},
        compiler_params=pltpu.CompilerParams(vmem_limit_bytes=VMEM_BYTES),
        cost_estimate=pl.CostEstimate(flops=flops, bytes_accessed=moved, transcendentals=0),
        name=kernel.__name__,
    )


def whole_block(shape):
    return pl.BlockSpec(shape, lambda g, core: (0,) * len(shape), pipeline_mode=pl.Buffered(1))


def by_core(core, near, far, axis):
    return jnp.where(
        core[0] == 0,
        jnp.concatenate([near, far], axis=axis),
        jnp.concatenate([far, near], axis=axis),
    )


def norm_kernel(core, tokens, gain_one, shift_one, gain_two, shift_two, na, nm, na_t, nm_t):
    inputs = tokens[...].astype(f32)
    centre = inputs - jnp.mean(inputs, axis=-1, keepdims=True)
    spread = jnp.mean(centre * centre, axis=-1, keepdims=True)
    normed = centre * lax.rsqrt(spread + norm_eps)
    one = (normed * gain_one[...] + shift_one[...]).astype(bf16)
    two = (normed * gain_two[...] + shift_two[...]).astype(bf16)
    na[...], nm[...], na_t[...], nm_t[...] = one, two, one.T, two.T


def norms(core, tokens, rows):
    length = tokens.shape[0]
    tile = pl.BlockSpec((TOKEN_TILE, D), lambda g, core: (g, 0))
    turned = pl.BlockSpec((D, TOKEN_TILE), lambda g, core: (0, g))
    sd = jax.ShapeDtypeStruct
    return call(
        norm_kernel, (length // TOKEN_TILE,), [tile] + [whole_block((1, D))] * 4,
        [tile, tile, turned, turned],
        [sd((length, D), bf16)] * 2 + [sd((D, length), bf16)] * 2,
        (tokens,) + rows, flops=10**7, moved=10**7,
    )(core, tokens, *rows)


def attention_kernel(
    core, start, cos, sin, na_t, cot, wq, wk, wv, wo_near, wo_far, bq, bk, bv,
    grads, merged, gq_out, gk_out, gv_out, sum_q, sum_k, sum_v,
    bias, merged_t, gq_t, gk_t, gv_t, acc_k, acc_v,
):
    length = cot.shape[0]
    step = pl.program_id(0)

    @pl.when(step == 0)
    def _():
        key = lax.broadcasted_iota(jnp.int32, (length, length), 0)
        query = lax.broadcasted_iota(jnp.int32, (length, length), 1)
        bias[...] = jnp.where((key >= start[...]) & (key <= query), 0.0, -1e30)

    c, s = cos[...], sin[...]

    def project(w, b):
        return mul(w[...], na_t[...], 0, 0) + b[...]

    def rotate(v, sign):
        rows = []
        for h in range(HEADS_STEP):
            at = h * HEAD_DIM
            lo, hi = v[at : at + 8], v[at + 8 : at + 16]
            rows += [lo * c - sign * (hi * s), hi * c + sign * (lo * s), v[at + 16 : at + HEAD_DIM]]
        return jnp.concatenate(rows, axis=0)

    scale = HEAD_DIM**-0.5
    q_t = rotate(project(wq, bq), 1.0).astype(bf16) * jnp.asarray(scale, bf16)
    k_t = rotate(project(wk, bk), 1.0).astype(bf16)
    v_t = project(wv, bv).astype(bf16)
    gm_t = mul(by_core(core, wo_near[...], wo_far[...], 1), cot[...], 1, 1).astype(bf16)
    k, v = k_t.T, v_t.T
    for h in range(HEADS_STEP):
        hs = slice(h * HEAD_DIM, (h + 1) * HEAD_DIM)
        acc_k[...] = jnp.zeros_like(acc_k)
        acc_v[...] = jnp.zeros_like(acc_v)
        for i in range(length // QUERY_ROWS):
            n = QUERY_ROWS * (i + 1)
            qs = slice(i * QUERY_ROWS, n)
            scores = mul(k[:n, hs], q_t[hs, qs], 1, 0) + bias[:n, qs]
            weights = jnp.exp(scores - jnp.max(scores, axis=0, keepdims=True))
            probs = weights * (1.0 / jnp.sum(weights, axis=0, keepdims=True))
            probs_low = probs.astype(bf16)
            merged_t[hs, qs] = mul(v_t[hs, :n], probs_low, 1, 0).astype(bf16)
            grad_probs = mul(v[:n, hs], gm_t[hs, qs], 1, 0)
            inner = jnp.sum(grad_probs * probs, axis=0, keepdims=True)
            grad_scores = (probs * (grad_probs - inner)).astype(bf16)
            gq_t[hs, qs] = mul(k_t[hs, :n], grad_scores, 1, 0) * scale
            acc_k[:, :n] += mul(q_t[hs, qs], grad_scores, 1, 1)
            acc_v[:, :n] += mul(gm_t[hs, qs], probs_low, 1, 1)
        gk_t[hs, :] = acc_k[...]
        gv_t[hs, :] = acc_v[...]
    gq = rotate(gq_t[...], -1.0).astype(bf16)
    gk = rotate(gk_t[...], -1.0).astype(bf16)
    gv = gv_t[...].astype(bf16)
    column = pl.multiple_of(lax.rem(step, 2) * WIDTH, WIDTH)
    gq_out[...], gk_out[...], gv_out[...] = gq, gk, gv
    merged[pl.ds(column, WIDTH), :] = merged_t[...]
    for at, (part, out) in enumerate(((gq, sum_q), (gk, sum_k), (gv, sum_v))):
        out[...] = jnp.sum(part.astype(f32), axis=1, keepdims=True)
        grads[:, pl.ds(at * HALF + column, WIDTH)] = mul(na_t[...], part, 1, 1).astype(bf16)


def attention(core, last, start, cos, sin, na_t, cot, weights, near, far, bias_qkv):
    length = cot.shape[0]

    def at(core, g):
        return g + 2 * (core[0] if last else 1 - core[0])

    def columns(part):
        return pl.BlockSpec((D, WIDTH), lambda g, core: (0, 2 * part + g))

    def entries(part):
        return pl.BlockSpec((WIDTH, 1), lambda g, core: (4 * part + at(core, g), 0))

    sd = jax.ShapeDtypeStruct
    rows_of_out = pl.BlockSpec((WIDTH, HALF), lambda g, core: (at(core, g), 3))
    turned = pl.BlockSpec((WIDTH, length), lambda g, core: (g, 0))
    summed = pl.BlockSpec((WIDTH, 1), lambda g, core: (g, 0))
    args = (start, cos, sin, na_t, cot) + (weights,) * 3 + (near, far) + (bias_qkv,) * 3
    in_specs = [whole_block(a.shape) for a in args[:5]] + [columns(0), columns(1), columns(2)]
    in_specs += [rows_of_out] * 2 + [entries(0), entries(1), entries(2)]
    out_specs = [whole_block((D, 3 * HALF)), whole_block((HALF, length))]
    out_specs += [turned] * 3 + [summed] * 3
    out_shape = [sd((D, 3 * HALF), bf16)] + [sd((HALF, length), bf16)] * 4
    out_shape += [sd((HALF, 1), f32)] * 3
    return call(
        attention_kernel, (2,), in_specs, out_specs, out_shape, args,
        scratch=[
            pltpu.VMEM((length, length), f32),
            pltpu.VMEM((WIDTH, length), bf16),
            pltpu.VMEM((WIDTH, length), f32),
            pltpu.VMEM((WIDTH, length), f32),
            pltpu.VMEM((WIDTH, length), f32),
            pltpu.VMEM((HEAD_DIM, length), f32),
            pltpu.VMEM((HEAD_DIM, length), f32),
        ],
        flops=50 * 10**9, moved=2 * 10**7,
    )(core, *args)


def ffn_kernel(
    core, nm, cot, w_in, w_down, b_in, merged_near, merged_far, *refs, which
):
    far, near, active_out, grad_out, grad_b = refs[-5:]
    hidden = mul(nm[...], w_in[...], 1, 0) + b_in[...]
    cdf = 0.5 * (1.0 + lax.erf(hidden * (2.0**-0.5)))
    pdf = jnp.exp(-0.5 * hidden * hidden) * (1.0 / math.sqrt(2.0 * math.pi))
    active = (hidden * cdf).astype(bf16)
    grad_hidden = (mul(cot[...], w_down[...], 1, 1) * (cdf + hidden * pdf)).astype(bf16)
    active_out[...], grad_out[...] = active, grad_hidden
    grad_b[...] = jnp.sum(grad_hidden.astype(f32), axis=0, keepdims=True)
    blocks = far.shape[0]
    merged = jnp.where(core[0] == which, merged_near[...], merged_far[...])
    grad_down = mul(active, cot[...], 0, 0).astype(bf16).reshape(blocks, -1, D)
    grad_wo = mul(merged, cot[...], 1, 0).astype(bf16).reshape(blocks, -1, D)
    at, left = grad_down.shape[1], core[0] == 0
    for rows, grad in ((slice(0, at), grad_down), (slice(at, None), grad_wo)):
        far[:, rows, :] = jnp.where(left, grad[..., HALF:], grad[..., :HALF])
        near[:, rows, :] = jnp.where(left, grad[..., :HALF], grad[..., HALF:])


def ffn_first(*refs):
    ffn_kernel(*refs, which=0)


def ffn_second(*refs):
    ffn_kernel(*refs, which=1)


def ffn(core, which, blocks, nm, cot, w_in, w_down, b_in, merged, after, before=()):
    length = nm.shape[0]
    sd = jax.ShapeDtypeStruct
    steps = FF // FF_TILE // 2
    share = (blocks // (2 * steps), (FF + D) // blocks, HALF)
    columns = pl.BlockSpec((D, FF_TILE), lambda g, core: (0, steps * which + g))
    tall = pl.BlockSpec((length, FF_TILE), lambda g, core: (0, steps * which + g))
    row = pl.BlockSpec((1, FF_TILE), lambda g, core: (0, steps * which + g))
    wide = pl.BlockSpec((FF_TILE, D), lambda g, core: (steps * which + g, 0))
    heads = pl.BlockSpec((HALF // steps, length), lambda g, core: (g, 0))
    grads = pl.BlockSpec(share, lambda g, core: (steps * which + g, 0, 0))
    args = (nm, cot, w_in, w_down, b_in) + merged
    more = tuple(before) + tuple(after)
    return call(
        ffn_second if which else ffn_first, (steps,),
        [whole_block((length, D))] * 2 + [columns, wide, row, heads, heads],
        [grads, grads, tall, tall, row],
        [sd((blocks,) + share[1:], bf16)] * 2 + [sd((length, FF), bf16)] * 2 + [sd((1, FF), f32)],
        args, more, aliases={1 + len(args) + at: at for at in range(len(before))},
        flops=16 * 10**9, moved=3 * 10**7,
    )(core, *args, *more)


def grad_in_kernel(core, nm_t, grad_hidden, far, near):
    step = pl.program_id(0)
    half = pl.num_programs(0) // 2

    def store(ref):
        ref[...] = mul(nm_t[...], grad_hidden[...], 1, 0).astype(bf16)

    pl.when(step < half)(lambda: store(far))
    pl.when(step >= half)(lambda: store(near))


def grads_in(core, nm_t, grad_hidden, after):
    length = nm_t.shape[1]
    sd = jax.ShapeDtypeStruct
    half = FF // FF_TILE // 2
    args = (nm_t, grad_hidden)
    return call(
        grad_in_kernel, (2 * half,),
        [
            whole_block((D, length)),
            pl.BlockSpec(
                (length, FF_TILE), lambda g, core: (0, lax.rem(g + (1 - core[0]) * half, 2 * half))
            ),
        ],
        [
            pl.BlockSpec((D, FF_TILE), lambda g, core: (0, jnp.minimum(g, half - 1))),
            pl.BlockSpec((D, FF_TILE), lambda g, core: (0, jnp.maximum(g - half, 0))),
        ],
        [sd((D, FF // 2), bf16)] * 2, args, after, flops=9 * 10**9, moved=2 * 10**7,
    )(core, *args, *after)


def output_kernel(core, tokens, near_t, far_t, active, wo_near, wo_far, w_down, b_sum, output):
    merged_t = by_core(core, near_t[...], far_t[...], 0)
    att = by_core(core, mul(merged_t, wo_near[...], 0, 0), mul(merged_t, wo_far[...], 0, 0), 1)
    fed = mul(active[...], w_down[...], 1, 0)
    output[...] = (tokens[...].astype(f32) + att + fed + b_sum[...]).astype(bf16)


def outputs(core, tokens, near_t, far_t, active, near, far, w_down, b_sum, after):
    length = tokens.shape[0]
    tile = pl.BlockSpec((TOKEN_TILE, D), lambda g, core: (g, 0))
    turned = pl.BlockSpec((HALF, TOKEN_TILE), lambda g, core: (0, g))
    out_columns = pl.BlockSpec((D, HALF), lambda g, core: (0, 3), pipeline_mode=pl.Buffered(1))
    args = (tokens, near_t, far_t, active, near, far, w_down, b_sum)
    return call(
        output_kernel, (length // TOKEN_TILE,),
        [tile, turned, turned, pl.BlockSpec((TOKEN_TILE, FF), lambda g, core: (g, 0))]
        + [out_columns] * 2 + [whole_block((FF, D)), whole_block((1, D))],
        [tile], [jax.ShapeDtypeStruct((length, D), bf16)], args, after,
        flops=11 * 10**9, moved=3 * 10**7,
    )(core, *args, *after)[0]


def input_kernel(
    core, tokens, cot, gq_near, gk_near, gv_near, gq_far, gk_far, gv_far, grad_hidden,
    near, far, w_in, gain_one, gain_two, input_grad, sums,
):
    inputs = tokens[...].astype(f32)
    centre = inputs - jnp.mean(inputs, axis=-1, keepdims=True)
    spread = jnp.mean(centre * centre, axis=-1, keepdims=True)
    rstd = lax.rsqrt(spread + norm_eps)
    normed = centre * rstd
    joined_near = jnp.concatenate([gq_near[...], gk_near[...], gv_near[...]], axis=0)
    joined_far = jnp.concatenate([gq_far[...], gk_far[...], gv_far[...]], axis=0)
    grad_na = mul(joined_near, near[...], 0, 1) + mul(joined_far, far[...], 0, 1)
    grad_nm = mul(grad_hidden[...], w_in[...], 1, 1)
    grad_normed = grad_na * gain_one[...] + grad_nm * gain_two[...]
    cotangent = cot[...].astype(f32)
    input_grad[...] = cotangent + rstd * (
        grad_normed
        - jnp.mean(grad_normed, axis=-1, keepdims=True)
        - normed * jnp.mean(grad_normed * normed, axis=-1, keepdims=True)
    )

    @pl.when(pl.program_id(0) == 0)
    def _():
        sums[...] = jnp.zeros_like(sums)

    for at, terms in enumerate((cotangent, grad_na * normed, grad_na, grad_nm * normed, grad_nm)):
        sums[at : at + 1, :] += jnp.sum(terms, axis=0, keepdims=True)


def input_grads(core, tokens, cot, joined, grad_hidden, near, far, w_in, gains, after):
    length = tokens.shape[0]
    tile = pl.BlockSpec((TOKEN_TILE, D), lambda g, core: (g, 0))
    turned = pl.BlockSpec((HALF, TOKEN_TILE), lambda g, core: (0, g))
    share = pl.BlockSpec((D, 3 * HALF), lambda g, core: (0, 0), pipeline_mode=pl.Buffered(1))
    args = (tokens, cot) + joined + (grad_hidden, near, far, w_in) + gains
    sd = jax.ShapeDtypeStruct
    return call(
        input_kernel, (length // TOKEN_TILE,),
        [tile, tile] + [turned] * 6 + [pl.BlockSpec((TOKEN_TILE, FF), lambda g, core: (g, 0))]
        + [share] * 2 + [whole_block((D, FF))] + [whole_block((1, D))] * 2,
        [tile, whole_block((8, D))],
        [sd((length, D), f32), sd((8, D), f32)], args, after, flops=15 * 10**9, moved=4 * 10**7,
    )(core, *args, *after)


def round_kernel(core, value, low):
    low[...] = value[...].astype(bf16)


def rounded(core, value, after):
    block = whole_block(value.shape)
    low = jax.ShapeDtypeStruct(value.shape, bf16)
    return call(round_kernel, (1,), [block], [block], [low], (value,), after)(core, value, *after)[0]


def later(value, *after):
    return lax.optimization_barrier((value,) + after)[0]


class Links:
    def __init__(self, sizes):
        self.sizes = sizes
        self.nz = sizes["z"]
        self.every = tuple(sizes)

    def swap(self, axis, value, bit=1):
        return lax.ppermute(value, axis, [(i, i ^ bit) for i in range(self.sizes[axis])])

    def bits(self, axis):
        return [1 << i for i in range(self.sizes[axis].bit_length() - 1)]

    def total(self, value):
        for axis in self.every[::-1]:
            for bit in self.bits(axis):
                value = value + self.swap(axis, value, bit)
        return value

    def gather(self, value):
        x, y, z = (lax.axis_index(axis) for axis in "xyz")

        def ordered(at, own, other):
            return jnp.where(
                at == 0, jnp.concatenate([own, other]), jnp.concatenate([other, own])
            )

        column = value[None]
        for bit in self.bits("z")[:-1]:
            column = ordered(z // (2 * bit) % 2, column, self.swap("z", column, 2 * bit))
        other = self.swap("z", column)
        self.column = other
        even = jnp.where(z % 2 == 0, column, other)[:, None, None, None]
        odd = jnp.where(z % 2 == 0, other, column)[:, None, None, None]
        even_y, odd_x = self.swap("y", even), self.swap("x", odd)
        even = jnp.where(
            y == 0, jnp.concatenate([even, even_y], 2), jnp.concatenate([even_y, even], 2)
        )
        odd = jnp.where(
            x == 0, jnp.concatenate([odd, odd_x], 3), jnp.concatenate([odd_x, odd], 3)
        )
        even_x, odd_y = self.swap("x", even), self.swap("y", odd)
        whole = jnp.zeros((self.nz // 2, 2, 2, 2) + value.shape, value.dtype)
        for part, at in (
            (even, (0, 0, x)), (even_x, (0, 0, 1 - x)), (odd, (1, y, 0)), (odd_y, (1, 1 - y, 0))
        ):
            whole = lax.dynamic_update_slice(whole, part, (0,) + at + (0, 0))
        return whole.reshape(-1, value.shape[-1])

    def owners(self, held, core, parts=1):
        cuts = [held.shape[0] * 4 // 5] if parts == 2 else []
        mine, other = [], []
        for part in jnp.split(held, cuts):
            rows = part.shape[0] // 2
            mine.append(lax.dynamic_slice_in_dim(part, core * rows, rows))
            other.append(lax.dynamic_slice_in_dim(part, (1 - core) * rows, rows))
        mine = jnp.concatenate(mine)
        came = self.swap("c", jnp.concatenate(other))
        return jnp.concatenate(
            [jnp.where(core == 0, mine, came), jnp.where(core == 0, came, mine)], axis=1
        )


class Scatter:
    def __init__(self, links, near, came):
        self.links, split = links, (links.nz // 2, 2, 2, 2, -1, near.shape[-1])
        self.near, self.came = near.reshape(split), came.reshape(split)
        self.x, self.y, self.z = (lax.axis_index(axis) for axis in "xyz")
        self.first = (
            self.term(0, x=1 - self.x).astype(bf16),
            self.term(1, y=1 - self.y).astype(bf16),
        )

    def term(self, odd, y=None, x=None):
        def cut(v):
            v = v[:, odd]
            if x is not None:
                v = lax.dynamic_index_in_dim(v, x, 2, False)
            if y is not None:
                v = lax.dynamic_index_in_dim(v, y, 1, False)
            return v.astype(f32)

        return cut(self.near) + cut(self.came)

    def came_at(self, part, at):
        return lax.dynamic_index_in_dim(part, at, 1, False).astype(f32)

    def step_one(self, *after):
        even, odd = self.links.swap("x", self.first[0]), self.links.swap("y", self.first[1])
        self.even, self.odd = later((even, odd), *after)
        x, y = self.x, self.y
        self.second = (
            (self.term(0, 1 - y, x) + self.came_at(self.even, 1 - y)).astype(bf16),
            (self.term(1, y, 1 - x) + self.came_at(self.odd, 1 - x)).astype(bf16),
        )

    def step_two(self, *after):
        even, odd = self.links.swap("y", self.second[0]), self.links.swap("x", self.second[1])
        even, odd = later((even, odd), *after)
        x, y = self.x, self.y
        even = self.term(0, y, x) + self.came_at(self.even, y) + even.astype(f32)
        odd = self.term(1, y, x) + self.came_at(self.odd, x) + odd.astype(f32)
        low = self.z % 2 == 0
        self.keep, self.send = jnp.where(low, even, odd), jnp.where(low, odd, even).astype(bf16)

    def finish(self, *after):
        came = later(self.links.swap("z", self.send), *after) if after else self.links.swap("z", self.send)
        held = self.keep + came.astype(f32)
        for bit in self.links.bits("z")[:-1][::-1]:
            mine = self.z // (2 * bit) % 2
            send = lax.dynamic_slice_in_dim(held, (1 - mine) * bit, bit).astype(bf16)
            keep = lax.dynamic_slice_in_dim(held, mine * bit, bit)
            held = keep + self.links.swap("z", send, 2 * bit).astype(f32)
        return held[0]


def per_device(
    links,
    tokens,
    cotangent,
    doc_ids,
    w_qkv,
    w_out,
    w_in,
    w_down,
    vectors,
    first_qkv,
    first_out,
    first_in,
    first_down,
    first_vectors,
    second_qkv,
    second_out,
    second_in,
    second_down,
    second_vectors,
):
    every = links.every
    core = lax.axis_index("c")
    core_ref = core.astype(jnp.int32).reshape(1)
    length = tokens.shape[0]
    rows = w_qkv.shape[0]
    per_row = vectors.shape[0] // rows

    spare = jnp.pad(vectors.astype(bf16).reshape(rows, per_row), ((0, 0), (0, 128 - per_row)))
    halves = jnp.concatenate([w_qkv, w_out], axis=1).astype(bf16).reshape(rows, 4, 2, HALF)

    def share(at):
        part = lax.dynamic_index_in_dim(halves, at, 2, False).reshape(rows, 4 * HALF)
        return jnp.concatenate([part, spare], axis=1)

    mine, came = share(core), links.swap("c", share(1 - core))
    near = links.gather(
        jnp.where(core == 0, jnp.concatenate([mine, came]), jnp.concatenate([came, mine]))
    )
    far = links.swap("c", near)
    w_in_all = lax.all_gather(rounded(core_ref, w_in, (links.column,)), every, axis=0, tiled=True)
    w_down_all = lax.all_gather(rounded(core_ref, w_down, (links.column,)), every, axis=0, tiled=True)
    vector_all = near[:, 4 * HALF : 4 * HALF + per_row].reshape(-1).astype(f32)
    b_qkv, b_out, b_in, b_down, gain_one, shift_one, gain_two, shift_two = split_vector(vector_all)

    positions = positions_of(doc_ids)
    start = (jnp.arange(length, dtype=jnp.int32) - positions).reshape(1, length)
    freqs = jnp.exp(jnp.arange(ROT // 2, dtype=f32) * (-2.0 * math.log(10000.0) / ROT))
    angles = freqs[:, None] * positions.astype(f32)[None, :]
    gains = (gain_one.reshape(1, D), gain_two.reshape(1, D))
    na, nm, na_t, nm_t = norms(
        core_ref, tokens, (gains[0], shift_one.reshape(1, D), gains[1], shift_two.reshape(1, D))
    )
    common = (start, jnp.cos(angles), jnp.sin(angles), na_t, cotangent)
    bias_qkv = b_qkv.reshape(3 * D, 1)
    grads_far, merged_far, *joined_far = attention(
        core_ref, False, *common, far, near, far, bias_qkv
    )
    came_heads = links.swap("c", grads_far)
    grads_near, merged_near, *joined_near = attention(
        core_ref, True, *common, near, near, far, bias_qkv
    )
    heads = Scatter(links, grads_near, came_heads)
    blocks = D // rows // 2
    fixed = (nm, cotangent, w_in_all, w_down_all, b_in.reshape(1, FF), (merged_near, merged_far))
    filled = ffn(core_ref, 0, blocks, *fixed, heads.first)
    heads.step_one(filled[4])
    down_far, down_near, active, grad_hidden, sum_in = ffn(
        core_ref, 1, blocks, *fixed, heads.second, filled
    )
    came_down = links.swap("c", down_far)
    heads.step_two(sum_in)
    in_far, in_near = grads_in(core_ref, nm_t, grad_hidden, (heads.send,))
    came_in = links.swap("c", in_far)
    down = Scatter(links, down_near, came_down)
    output = outputs(
        core_ref, tokens, merged_near, merged_far, active, near, far, w_down_all,
        (b_out + b_down).reshape(1, D), down.first,
    )
    grad_heads = links.owners(heads.finish(output[:8, :128]), core)
    inner = Scatter(links, in_near, came_in)
    down.step_one(output[:8, :128])
    input_grad, sums = input_grads(
        core_ref, tokens, cotangent, tuple(joined_near[:3] + joined_far[:3]), grad_hidden,
        near, far, w_in_all, gains, down.second + inner.first + (output,),
    )
    heads_sums = [
        part[:, 0]
        for mine, other in zip(joined_near[3:], joined_far[3:])
        for part in (jnp.where(core == 0, mine, other), jnp.where(core == 0, other, mine))
    ]
    vector_terms = jnp.concatenate(
        heads_sums + [sums[0], sum_in[0], sums[0], sums[1], sums[2], sums[3], sums[4]]
    )
    vector_total = links.total(vector_terms.reshape(-1, 128)).reshape(-1)
    count_own = vectors.shape[0]
    grad_vectors = lax.dynamic_slice_in_dim(
        vector_total, lax.axis_index(every) * count_own, count_own
    )
    grad_qkv = grad_heads.reshape(rows, 2, 3, HALF).transpose(0, 2, 1, 3).reshape(rows, 3 * D)
    down.step_two(sums)
    inner.step_one(sums)
    grad_rows = links.owners(down.finish(), core, 2)
    grad_down, grad_out = grad_rows[: 4 * rows], grad_rows[4 * rows :]
    inner.step_two()
    grad_in = links.owners(inner.finish(), core)
    pieces = (grad_qkv, grad_out, grad_in, grad_down, grad_vectors)
    local_square = sum(jnp.sum(piece * piece) for piece in pieces)
    norm = jnp.sqrt(links.total(jnp.broadcast_to(local_square, (8, 128)))[0, 0])
    clip = jnp.minimum(1.0, clip_limit / (norm + 1e-06))
    masters = (w_qkv, w_out, w_in, w_down, vectors)
    firsts = (first_qkv, first_out, first_in, first_down, first_vectors)
    seconds = (second_qkv, second_out, second_in, second_down, second_vectors)
    results = [
        adam_step(w, g, f, s, clip, float(STEPS))
        for w, g, f, s in zip(masters, pieces, firsts, seconds)
    ]
    return (output, input_grad, norm.reshape(1)) + pieces + tuple(
        result[at] for at in range(3) for result in results
    )


def solution(mesh):
    fsdp, rep = mesh.shape["fsdp"], mesh.shape["rep"]
    sizes = {"z": fsdp // 2, "y": 2, "x": rep // 2, "c": 2}
    cut = Mesh(mesh.devices.reshape(tuple(sizes.values())), tuple(sizes))
    names = tuple(sizes)
    wide, flat = P(names, None), P(names)
    group = (wide, wide, wide, wide, flat)
    body = jax.shard_map(
        functools.partial(per_device, Links(sizes)),
        mesh=cut,
        in_specs=(wide, wide, flat) + group * 3,
        out_specs=(wide, wide, P()) + group * 4,
        check_vma=False,
    )
    return body
```

time: 1170 us -> 546 us (0.47); the launches traced: 1160 us -> 545 us
  matrix products: 438 us -> 0 us
  waiting for transfers between devices: 392 us -> 149 us
  Pallas kernels: 0 us -> 227 us
  blocking collectives: 128 us -> 0 us
  local copies, waits for them, and re-layouts: 92.6 us -> 46.4 us
  starting transfers between devices: 0.33 us -> 45.5 us
  other arithmetic: 85.2 us -> 56.9 us
    dot_general x124 -> x0, matrix products: 438 us -> none  [the longest x16 60.4 us: head_forward(): jnp.dot(probs.astype(jnp.bfloat16), value, preferred_element_type=jnp.flo...]
    reduce_scatter x4 -> x0, waiting for transfers between devices: 325 us -> none  [the longest x1 185 us: per_device(): lax.psum_scatter(grad_down_w, ('fsdp', 'rep'), scatter_dimension=0, tiled...]
    pallas_call x0 -> x10, Pallas kernels: none -> 227 us  [the longest x2 111 us: attention(): call(attention_kernel, (2,), in_specs, out_specs, out_shape, args, scratc...]
    ppermute x0 -> x42, waiting for transfers between devices: none -> 149 us  [swap(): lax.ppermute(value, axis, [(i, i ^ bit) for i in range(self.sizes[axis])])]
    unnamed x2 -> x0, blocking collectives: 85.7 us -> none
    all_gather x4 -> x2, waiting for transfers between devices: 66 us -> 0.01 us  [the longest x1 0.01 us: per_device(): lax.all_gather(rounded(core_ref, w_in, (links.column,)), every, axis=0, t...]
    ppermute x0 -> x42, starting transfers between devices: none -> 45.4 us  [swap(): lax.ppermute(value, axis, [(i, i ^ bit) for i in range(self.sizes[axis])])]
    psum x1 -> x0, blocking collectives: 42.4 us -> none  [per_device(): total_square = lax.psum(local_square, ('fsdp', 'rep'))]
  transfers between devices with their start and end apart: 8 -> 44, of which waited for: 4 -> 20; matrix products, arithmetic and copies ran while one was open for 47% -> 15% of each run, Pallas kernels for 0% -> 39%
where the time goes in v1:
time: 546 us; the launch traced here: 545 us
  Pallas kernels  227 us (42%)
  waiting for transfers between devices  149 us (27%)
  other arithmetic  56.9 us (10%)
  local copies, waits for them, and re-layouts  46.4 us (8%)
  starting transfers between devices  45.5 us (8%)
  between operations  20.5 us (4%)
    ppermute x42, waiting for transfers between devices, swap(): lax.ppermute(value, axis, [(i, i ^ bit) for i in range(self.sizes[axis])])  149 us
    pallas_call x2, Pallas kernels, attention(): call(attention_kernel, (2,), in_specs, out_specs, out_shape, args, scratc...  111 us
    pallas_call x2, Pallas kernels, ffn(): call(ffn_second if which else ffn_first, (steps,), [whole_block((length,...  45.8 us
    ppermute x42, starting transfers between devices, swap(): lax.ppermute(value, axis, [(i, i ^ bit) for i in range(self.sizes[axis])])  45.4 us
    pallas_call x1, Pallas kernels, input_grads(): call(input_kernel, (length // TOKEN_TILE,), [tile, tile] + [turned] * 6 +...  27.7 us
    slice x6, local copies, waits for them, and re-layouts, cut(): v = v[:, odd]  18 us
    pallas_call x1, Pallas kernels, outputs(): call(output_kernel, (length // TOKEN_TILE,), [tile, turned, turned, pl.Bl...  17.8 us
    pallas_call x1, Pallas kernels, grads_in(): call(grad_in_kernel, (2 * half,), [whole_block((D, length)), pl.BlockSpec...  14.8 us
  transfers between devices with their start and end apart: 44, of which 20 were waited for; matrix products, arithmetic and copies ran while one was open for 15% of the time, Pallas kernels for 39%

profile of v1, /device:TPU:0, one launch (start us, length us, event | category | flops | bytes accessed | tf_op | source)
XLA Modules:
  0.0 545.4 jit_solution(17639636144283785176)
XLA Ops:
  12.8 4.0 collective-permute-start.1
  16.9 12.9 %collective-permute-done.1 = bf16[1,64,2176]{2,1,0:T(8,128)(2,1)S(1)} collective-permute-done((bf16[1,64,2176]{2,1,0:T(8,128)(2,1)S(1)}, bf16[1,64,2176]{2,1,0:T(8,128)(2,1)S(1)}, u32[]{:S(2)}, u32[]{:S(2)}) %collective-permute-start.1) | collective-permute-done | bytes 278560 | tf_op jit(solution)/shard_map/ppermute | solution.py:398
  30.7 13.4 %collective-permute-done.2.refs_2_ = bf16[2,64,2176]{2,1,0:T(8,128)(2,1)S(1)} collective-permute-done((bf16[2,64,2176]{2,1,0:T(8,128)(2,1)S(1)}, bf16[2,64,2176]{2,1,0:T(8,128)(2,1)S(1)}, u32[]{:S(2)}, u32[]{:S(2)}) %collective-permute-start.2) | collective-permute-done | bytes 557088 | tf_op jit(solution)/shard_map/ppermute | solution.py:398
  50.8 12.4 %collective-permute-done.3 = bf16[2,1,1,1,64,2176]{5,4,0,3,2,1:T(8,128)(2,1)S(1)} collective-permute-done((bf16[2,1,1,1,64,2176]{5,4,0,3,2,1:T(8,128)(2,1)S(1)}, bf16[2,1,1,1,64,2176]{5,4,0,3,2,1:T(8,128)(2,1)S(1)}, u32[]{:S(2)}, u32[]{:S(2)}) %collective-permute-start.3) | collective-permute-done | bytes 557088 | tf_op jit(solution)/shard_map/ppermute | solution.py:398
  72.7 22.5 %collective-permute-done.4 = bf16[2,1,2,1,64,2176]{5,4,0,3,2,1:T(8,128)(2,1)S(1)} collective-permute-done((bf16[2,1,2,1,64,2176]{5,4,0,3,2,1:T(8,128)(2,1)}, bf16[2,1,2,1,64,2176]{5,4,0,3,2,1:T(8,128)(2,1)S(1)}, u32[]{:S(2)}, u32[]{:S(2)}) %collective-permute-start.4) | collective-permute-done | bytes 1114144 | tf_op jit(solution)/shard_map/ppermute | solution.py:398
  105.0 6.1 %norm_kernel.1 = (bf16[1024,1024]{1,0:T(8,128)(2,1)}, bf16[1024,1024]{1,0:T(8,128)(2,1)}, bf16[1024,1024]{1,0:T(8,128)(2,1)}, bf16[1024,1024]{1,0:T(8,128)(2,1)}) custom-call(s32[1]{0:T(128)} %bitcast.refs_0_, bf16[1024,1024]{1,0:T(8,128)(2,1)} %refs_1_.9, f32[1,1024]{1,0:T(1,128)} %bitcast.300, f32[1,1024]{1,0:T(1,128)} %bitcast.303, f32[1,1024]{1,0:T(1,128)} %bitcast.298, ...), custom_call_target="tpu_custom_call" | custom-call | flops 10000000 | bytes 10000000 | tf_op jit(solution)/shard_map/norm_kernel/pallas_call | solution.py:116
  111.1 49.3 %attention_kernel.3 = (bf16[1024,1536]{1,0:T(8,128)(2,1)}, bf16[512,1024]{1,0:T(8,128)(2,1)}, bf16[512,1024]{1,0:T(8,128)(2,1)}, bf16[512,1024]{1,0:T(8,128)(2,1...) custom-call(s32[1]{0:T(128)} %bitcast.refs_0_, ...), custom_call_target="tpu_custom_call" | custom-call | flops 49999998976 | bytes 20000000 | tf_op jit(solution)/shard_map/attention_kernel/pallas_call | solution.py:211
  161.0 61.7 %attention_kernel.2 = (bf16[1024,1536]{1,0:T(8,128)(2,1)}, bf16[512,1024]{1,0:T(8,128)(2,1)}, bf16[512,1024]{1,0:T(8,128)(2,1)}, bf16[512,1024]{1,0:T(8,128)(2,1...) custom-call(s32[1]{0:T(128)} %bitcast.refs_0_, ...), custom_call_target="tpu_custom_call" | custom-call | flops 49999998976 | bytes 20000000 | tf_op jit(solution)/shard_map/attention_kernel/pallas_call | solution.py:211
  224.9 3.2 fusion.39
  236.5 22.8 %ffn_first.1 = (bf16[16,320,512]{2,1,0:T(8,128)(2,1)}, bf16[16,320,512]{2,1,0:T(8,128)(2,1)}, bf16[1024,4096]{1,0:T(8,128)(2,1)}, bf16[1024,4096]{1,0:T(8,128)(2,1)}, f32[1,4096]{1,0:T(1,128)}) custom-call(s32[1]{0:T(128)} %bitcast.refs_0_, bf16[1024,1024]{1,0:T(8,128)(2,1)} %get-tuple-element.72.refs_1_, bf16[1024,1024]{1,0:T(8,128)(2,1)} %refs_2_.5, ...), custom_call_target="tpu_custom_call" | custom-call | flops 16000000000 | bytes 30000000 | tf_op jit(solution)/shard_map/ffn_first/pallas_call | solution.py:268
  264.7 23.0 %ffn_second.1 = (bf16[16,320,512]{2,1,0:T(8,128)(2,1)}, bf16[16,320,512]{2,1,0:T(8,128)(2,1)}, bf16[1024,4096]{1,0:T(8,128)(2,1)}, bf16[1024,4096]{1,0:T(8,128)(2,1)}, f32[1,4096]{1,0:T(1,128)}) custom-call(s32[1]{0:T(128)} %bitcast.refs_0_, ...), custom_call_target="tpu_custom_call", output_to_operand_aliasing={{0}: (8, {}), {1}: (9, {}), {2}: (10, {}), {3}: (11, {}), {... | custom-call | flops 16000000000 | bytes 30000000 | tf_op jit(solution)/shard_map/ffn_second/pallas_call | solution.py:268
  290.4 14.8 %grad_in_kernel.1 = (bf16[1024,2048]{1,0:T(8,128)(2,1)}, bf16[1024,2048]{1,0:T(8,128)(2,1)}) custom-call(s32[1]{0:T(128)} %bitcast.refs_0_, bf16[1024,1024]{1,0:T(8,128)(2,1)} %get-tuple-element.94.refs_1_, bf16[1024,4096]{1,0:T(8,128)(2,1)} %get-tuple-element.91.refs_2_.refs_9_, bf16[2,64,1536]{2,1,0:T(8,128)(2,1)} %select_convert_fusion.2.refs_3_), custom_call_target="tpu_custom_call" | custom-call | flops 8999999488 | bytes 20000000 | tf_op jit(solution)/shard_map/grad_in_kernel/pallas_call | solution.py:294
  313.4 4.8 fusion.37
  334.6 17.8 %output_kernel.1.refs_19_ = bf16[1024,1024]{1,0:T(8,128)(2,1)} custom-call(s32[1]{0:T(128)} %bitcast.refs_0_, bf16[1024,1024]{1,0:T(8,128)(2,1)} %refs_1_.9, bf16[512,1024]{1,0:T(8,128)(2,1)} %get-tuple-element.70.refs_6_.refs_2_, bf16[512,1024]{1,0:T(8,128)(2,1)} %get-tuple-element.71.refs_7_.refs_3_, bf16[1024,4096]{1,0:T(8,128)(2,1)} %get-tuple-element.82.refs_4_, ...), custom_call_target="tpu_custom_call" | custom-call | flops 11000000512 | bytes 30000000 | tf_op jit(solution)/shard_map/output_kernel/pallas_call | solution.py:323
  354.8 3.9 collective-permute-start.18
  362.5 5.0 collective-permute-done.18
  371.1 20.7 %collective-permute-done.13 = bf16[2,2,320,512]{3,2,0,1:T(8,128)(2,1)S(1)} collective-permute-done((bf16[2,2,320,512]{3,2,0,1:T(8,128)(2,1)S(1)}, bf16[2,2,320,512]{3,2,0,1:T(8,128)(2,1)S(1)}, u32[]{:S(2)}, u32[]{:S(2)}) %collective-permute-start.13) | collective-permute-done | bytes 1310752 | tf_op jit(solution)/shard_map/ppermute | solution.py:398
  396.6 27.7 %input_kernel.1 = (f32[1024,1024]{1,0:T(8,128)}, f32[8,1024]{1,0:T(8,128)}) custom-call(s32[1]{0:T(128)} %bitcast.refs_0_, bf16[1024,1024]{1,0:T(8,128)(2,1)} %refs_1_.9, bf16[1024,1024]{1,0:T(8,128)(2,1)} %refs_2_.5, bf16[512,1024]{1,0:T(8,128)(2,1)} %get-tuple-element.85.refs_3_, bf16[512,1024]{1,0:T(8,128)(2,1)} %get-tuple-element.86.refs_4_, ...), custom_call_target="tpu_custom_call" | custom-call | flops 15000000512 | bytes 40000000 | tf_op jit(solution)/shard_map/input_kernel/pallas_call | solution.py:368
  434.4 9.1 %collective-permute-done.33 = f32[104,128]{1,0:T(8,128)S(1)} collective-permute-done((f32[104,128]{1,0:T(8,128)S(1)}, f32[104,128]{1,0:T(8,128)S(1)}, u32[]{:S(2)}, u32[]{:S(2)}) %collective-permute-start.33) | collective-permute-done | bytes 53280 | tf_op jit(solution)/shard_map/ppermute | solution.py:398
  460.7 6.4 %collective-permute-done.21 = bf16[2,320,512]{2,1,0:T(8,128)(2,1)S(1)} collective-permute-done((bf16[2,320,512]{2,1,0:T(8,128)(2,1)}, bf16[2,320,512]{2,1,0:T(8,128)(2,1)S(1)}, u32[]{:S(2)}, u32[]{:S(2)}) %collective-permute-start.21) | collective-permute-done | bytes 655392 | tf_op jit(solution)/shard_map/ppermute | solution.py:398
  475.7 13.8 %collective-permute-done.22 = bf16[2,320,512]{2,1,0:T(8,128)(2,1)S(1)} collective-permute-done((bf16[2,320,512]{2,1,0:T(8,128)(2,1)S(1)}, bf16[2,320,512]{2,1,0:T(8,128)(2,1)S(1)}, u32[]{:S(2)}, u32[]{:S(2)}) %collective-permute-start.22) | collective-permute-done | bytes 655392 | tf_op jit(solution)/shard_map/ppermute | solution.py:398
  491.7 14.1 %collective-permute-done.23 = bf16[1,320,512]{2,1,0:T(8,128)(2,1)S(1)} collective-permute-done((bf16[1,320,512]{2,1,0:T(8,128)(2,1)S(1)}, bf16[1,320,512]{2,1,0:T(8,128)(2,1)S(1)}, u32[]{:S(2)}, u32[]{:S(2)}) %collective-permute-start.23) | collective-permute-done | bytes 327712 | tf_op jit(solution)/shard_map/ppermute | solution.py:398
  520.9 3.6 collective-permute-done.40
  525.3 3.7 collective-permute-done.41
  (312 shorter events, 148.1 us)
Async XLA Ops:
  7.2 229.3 %all-gather.3.cloned.1.call-start = ((), (), s32[]{:S(2)}) async-start(), calls=%async_computation | async-start | bytes 8650752 | tf_op jit(solution)/shard_map/all_gather | solution.py:546
  12.8 16.9 %collective-permute-start.1 = (bf16[1,64,2176]{2,1,0:T(8,128)(2,1)S(1)}, bf16[1,64,2176]{2,1,0:T(8,128)(2,1)S(1)}, u32[]{:S(2)}, u32[]{:S(2)}) collective-permute-start(bf16[1,64,2176]{2,1,0:T(8,128)(2,1)S(1)} %maximum_select_fusion.3), channel_id=1, source_target_pairs={{0,16},{8,24},{16,0},{24,8},{1,17},{9,25},{17,1},{25,9},{2,18},{10... | collective-permute-start | bytes 835592 | tf_op jit(solution)/shard_map/ppermute | solution.py:398
  46.7 189.8 %all-gather.5.cloned.1.call-start = ((), (), s32[]{:S(2)}) async-start(), calls=%async_computation.1 | async-start | bytes 8650752 | tf_op jit(solution)/shard_map/all_gather | solution.py:547
  48.0 15.2 %collective-permute-start.3 = (bf16[2,1,1,1,64,2176]{5,4,0,3,2,1:T(8,128)(2,1)S(1)}, bf16[2,1,1,1,64,2176]{5,4,0,3,2,1:T(8,128)(2,1)S(1)}, u32[]{:S(2)}, u32[]{:S(2)}) collective-permute-start(bf16[2,1,1,1,64,2176]{5,4,0,3,2,1:T(8,128)(2,1)S(1)} %get-tuple-element.161), channel_id=1, source_target_pairs={{0,4},{4,0},{1,5},{5,1},{2,6},{6,2},{3,7},{7,3},{8,12},{12,8},{9,1... | collective-permute-start | bytes 1671176 | tf_op jit(solution)/shard_map/ppermute | solution.py:398
  49.3 17.7 %collective-permute-start.5 = (bf16[2,1,1,1,64,2176]{5,4,0,3,2,1:T(8,128)(2,1)S(1)}, bf16[2,1,1,1,64,2176]{5,4,0,3,2,1:T(8,128)(2,1)S(1)}, u32[]{:S(2)}, u32[]{:S(2)}) collective-permute-start(bf16[2,1,1,1,64,2176]{5,4,0,3,2,1:T(8,128)(2,1)S(1)} %get-tuple-element.160), channel_id=1, source_target_pairs={{0,2},{2,0},{1,3},{3,1},{4,6},{6,4},{5,7},{7,5},{8,10},{10,8},{9,1... | collective-permute-start | bytes 1671176 | tf_op jit(solution)/shard_map/ppermute | solution.py:398
  64.4 30.8 %collective-permute-start.4 = (bf16[2,1,2,1,64,2176]{5,4,0,3,2,1:T(8,128)(2,1)}, bf16[2,1,2,1,64,2176]{5,4,0,3,2,1:T(8,128)(2,1)S(1)}, u32[]{:S(2)}, u32[]{:S(2)}) collective-permute-start(bf16[2,1,2,1,64,2176]{5,4,0,3,2,1:T(8,128)(2,1)} %maximum_select_fusion), channel_id=1, source_target_pairs={{0,2},{2,0},{1,3},{3,1},{4,6},{6,4},{5,7},{7,5},{8,10},{10,8},{9,1... | collective-permute-start | bytes 3342344 | tf_op jit(solution)/shard_map/ppermute | solution.py:398
  67.2 30.3 %collective-permute-start.6 = (bf16[2,1,1,2,64,2176]{5,4,0,3,2,1:T(8,128)(2,1)S(1)}, bf16[2,1,1,2,64,2176]{5,4,0,3,2,1:T(8,128)(2,1)S(1)}, u32[]{:S(2)}, u32[]{:S(2)}) collective-permute-start(bf16[2,1,1,2,64,2176]{5,4,0,3,2,1:T(8,128)(2,1)S(1)} %maximum_select_fusion.1), channel_id=1, source_target_pairs={{0,4},{4,0},{1,5},{5,1},{2,6},{6,2},{3,7},{7,3},{8,12},{12,8},{9,1... | collective-permute-start | bytes 3342344 | tf_op jit(solution)/shard_map/ppermute | solution.py:398
  160.5 64.4 %collective-permute-start.8 = (bf16[1024,1536]{1,0:T(8,128)(2,1)}, bf16[1024,1536]{1,0:T(8,128)(2,1)}, u32[]{:S(2)}, u32[]{:S(2)}) collective-permute-start(bf16[1024,1536]{1,0:T(8,128)(2,1)} %get-tuple-element.74), channel_id=1, source_target_pairs={{0,1},{1,0},{2,3},{3,2},{4,5},{5,4},{6,7},{7,6},{8,9},{9,8},{10,11... | collective-permute-start | bytes 9437192 | tf_op jit(solution)/shard_map/ppermute | solution.py:398
  231.5 27.8 %collective-permute-start.10 = (bf16[2,2,64,1536]{3,2,0,1:T(8,128)(2,1)}, bf16[2,2,64,1536]{3,2,0,1:T(8,128)(2,1)}, u32[]{:S(2)}, u32[]{:S(2)}) collective-permute-start(bf16[2,2,64,1536]{3,2,0,1:T(8,128)(2,1)} %fusion.12), channel_id=1, source_target_pairs={{0,4},{4,0},{1,5},{5,1},{2,6},{6,2},{3,7},{7,3},{8,12},{12,8},{9,1... | collective-permute-start | bytes 2359304 | tf_op jit(solution)/shard_map/ppermute | solution.py:398
  235.7 23.5 %collective-permute-start.9 = (bf16[2,2,64,1536]{3,2,0,1:T(8,128)(2,1)}, bf16[2,2,64,1536]{3,2,0,1:T(8,128)(2,1)}, u32[]{:S(2)}, u32[]{:S(2)}) collective-permute-start(bf16[2,2,64,1536]{3,2,0,1:T(8,128)(2,1)} %fusion.11), channel_id=1, source_target_pairs={{0,2},{2,0},{1,3},{3,1},{4,6},{6,4},{5,7},{7,5},{8,10},{10,8},{9,1... | collective-permute-start | bytes 2359304 | tf_op jit(solution)/shard_map/ppermute | solution.py:398
  260.5 27.3 %collective-permute-start.15 = (bf16[2,64,1536]{2,1,0:T(8,128)(2,1)S(1)}, bf16[2,64,1536]{2,1,0:T(8,128)(2,1)S(1)}, u32[]{:S(2)}, u32[]{:S(2)}) collective-permute-start(bf16[2,64,1536]{2,1,0:T(8,128)(2,1)S(1)} %fusion.15.refs_14_), channel_id=1, source_target_pairs={{0,2},{2,0},{1,3},{3,1},{4,6},{6,4},{5,7},{7,5},{8,10},{10,8},{9,1... | collective-permute-start | bytes 1179656 | tf_op jit(solution)/shard_map/ppermute | solution.py:398
  263.8 24.0 %collective-permute-start.14 = (bf16[2,64,1536]{2,1,0:T(8,128)(2,1)}, bf16[2,64,1536]{2,1,0:T(8,128)(2,1)S(1)}, u32[]{:S(2)}, u32[]{:S(2)}) collective-permute-start(bf16[2,64,1536]{2,1,0:T(8,128)(2,1)} %fusion.16.refs_13_), channel_id=1, source_target_pairs={{0,4},{4,0},{1,5},{5,1},{2,6},{6,2},{3,7},{7,3},{8,12},{12,8},{9,1... | collective-permute-start | bytes 1179656 | tf_op jit(solution)/shard_map/ppermute | solution.py:398
  305.3 19.5 %collective-permute-start.11 = (bf16[16,320,512]{2,1,0:T(8,128)(2,1)}, bf16[16,320,512]{2,1,0:T(8,128)(2,1)}, u32[]{:S(2)}, u32[]{:S(2)}) collective-permute-start(bf16[16,320,512]{2,1,0:T(8,128)(2,1)} %get-tuple-element.84), channel_id=1, source_target_pairs={{0,1},{1,0},{2,3},{3,2},{4,5},{5,4},{6,7},{7,6},{8,9},{9,8},{10,11... | collective-permute-start | bytes 15728648 | tf_op jit(solution)/shard_map/ppermute | solution.py:398
  309.6 42.8 %collective-permute-start.17 = (bf16[2,64,1536]{2,1,0:T(8,128)(2,1)}, bf16[2,64,1536]{2,1,0:T(8,128)(2,1)}, u32[]{:S(2)}, u32[]{:S(2)}) collective-permute-start(bf16[2,64,1536]{2,1,0:T(8,128)(2,1)} %select_convert_fusion.2.refs_3_), channel_id=1, source_target_pairs={{0,8},{8,0},{16,24},{24,16},{1,9},{9,1},{17,25},{25,17},{2,10},{10... | collective-permute-start | bytes 1179656 | tf_op jit(solution)/shard_map/ppermute | solution.py:398
  323.3 102.2 %collective-permute-start.25 = (bf16[2,2,64,2048]{3,2,0,1:T(8,128)(2,1)}, bf16[2,2,64,2048]{3,2,0,1:T(8,128)(2,1)}, u32[]{:S(2)}, u32[]{:S(2)}) collective-permute-start(bf16[2,2,64,2048]{3,2,0,1:T(8,128)(2,1)} %fusion.6), channel_id=1, source_target_pairs={{0,2},{2,0},{1,3},{3,1},{4,6},{6,4},{5,7},{7,5},{8,10},{10,8},{9,1... | collective-permute-start | bytes 3145736 | tf_op jit(solution)/shard_map/ppermute | solution.py:398
  360.0 31.7 %collective-permute-start.13 = (bf16[2,2,320,512]{3,2,0,1:T(8,128)(2,1)S(1)}, bf16[2,2,320,512]{3,2,0,1:T(8,128)(2,1)S(1)}, u32[]{:S(2)}, u32[]{:S(2)}) collective-permute-start(bf16[2,2,320,512]{3,2,0,1:T(8,128)(2,1)S(1)} %copy-done.15), channel_id=1, source_target_pairs={{0,4},{4,0},{1,5},{5,1},{2,6},{6,2},{3,7},{7,3},{8,12},{12,8},{9,1... | collective-permute-start | bytes 3932168 | tf_op jit(solution)/shard_map/ppermute | solution.py:398
  362.0 29.7 %collective-permute-start.12 = (bf16[2,2,320,512]{3,2,0,1:T(8,128)(2,1)S(1)}, bf16[2,2,320,512]{3,2,0,1:T(8,128)(2,1)S(1)}, u32[]{:S(2)}, u32[]{:S(2)}) collective-permute-start(bf16[2,2,320,512]{3,2,0,1:T(8,128)(2,1)S(1)} %copy-done.17), channel_id=1, source_target_pairs={{0,2},{2,0},{1,3},{3,1},{4,6},{6,4},{5,7},{7,5},{8,10},{10,8},{9,1... | collective-permute-start | bytes 3932168 | tf_op jit(solution)/shard_map/ppermute | solution.py:398
  369.0 56.4 %collective-permute-start.26 = (bf16[2,2,64,2048]{3,2,1,0:T(8,128)(2,1)}, bf16[2,2,64,2048]{3,2,1,0:T(8,128)(2,1)}, u32[]{:S(2)}, u32[]{:S(2)}) collective-permute-start(bf16[2,2,64,2048]{3,2,1,0:T(8,128)(2,1)} %copy_bitcast_fusion.refs_18_), channel_id=1, source_target_pairs={{0,4},{4,0},{1,5},{5,1},{2,6},{6,2},{3,7},{7,3},{8,12},{12,8},{9,1... | collective-permute-start | bytes 3145736 | tf_op jit(solution)/shard_map/ppermute | solution.py:398
  427.9 27.0 %collective-permute-start.28 = (bf16[2,64,2048]{2,1,0:T(8,128)(2,1)}, bf16[2,64,2048]{2,1,0:T(8,128)(2,1)}, u32[]{:S(2)}, u32[]{:S(2)}) collective-permute-start(bf16[2,64,2048]{2,1,0:T(8,128)(2,1)} %fusion.8), channel_id=1, source_target_pairs={{0,2},{2,0},{1,3},{3,1},{4,6},{6,4},{5,7},{7,5},{8,10},{10,8},{9,1... | collective-permute-start | bytes 1572872 | tf_op jit(solution)/shard_map/ppermute | solution.py:398
  432.4 22.5 %collective-permute-start.27 = (bf16[2,64,2048]{2,1,0:T(8,128)(2,1)}, bf16[2,64,2048]{2,1,0:T(8,128)(2,1)}, u32[]{:S(2)}, u32[]{:S(2)}) collective-permute-start(bf16[2,64,2048]{2,1,0:T(8,128)(2,1)} %fusion.9), channel_id=1, source_target_pairs={{0,4},{4,0},{1,5},{5,1},{2,6},{6,2},{3,7},{7,3},{8,12},{12,8},{9,1... | collective-permute-start | bytes 1572872 | tf_op jit(solution)/shard_map/ppermute | solution.py:398
  451.5 15.5 %collective-permute-start.21 = (bf16[2,320,512]{2,1,0:T(8,128)(2,1)}, bf16[2,320,512]{2,1,0:T(8,128)(2,1)S(1)}, u32[]{:S(2)}, u32[]{:S(2)}) collective-permute-start(bf16[2,320,512]{2,1,0:T(8,128)(2,1)} %fusion.4.refs_16_), channel_id=1, source_target_pairs={{0,2},{2,0},{1,3},{3,1},{4,6},{6,4},{5,7},{7,5},{8,10},{10,8},{9,1... | collective-permute-start | bytes 1966088 | tf_op jit(solution)/shard_map/ppermute | solution.py:398
  452.1 15.2 %collective-permute-start.20 = (bf16[2,320,512]{2,1,0:T(8,128)(2,1)}, bf16[2,320,512]{2,1,0:T(8,128)(2,1)S(1)}, u32[]{:S(2)}, u32[]{:S(2)}) collective-permute-start(bf16[2,320,512]{2,1,0:T(8,128)(2,1)} %fusion.5.refs_15_), channel_id=1, source_target_pairs={{0,4},{4,0},{1,5},{5,1},{2,6},{6,2},{3,7},{7,3},{8,12},{12,8},{9,1... | collective-permute-start | bytes 1966088 | tf_op jit(solution)/shard_map/ppermute | solution.py:398
  469.6 20.0 %collective-permute-start.22 = (bf16[2,320,512]{2,1,0:T(8,128)(2,1)S(1)}, bf16[2,320,512]{2,1,0:T(8,128)(2,1)S(1)}, u32[]{:S(2)}, u32[]{:S(2)}) collective-permute-start(bf16[2,320,512]{2,1,0:T(8,128)(2,1)S(1)} %select_convert_fusion), channel_id=1, source_target_pairs={{0,8},{8,0},{16,24},{24,16},{1,9},{9,1},{17,25},{25,17},{2,10},{10... | collective-permute-start | bytes 1966088 | tf_op jit(solution)/shard_map/ppermute | solution.py:398
  473.4 18.1 %collective-permute-start.30 = (bf16[1,64,2048]{2,1,0:T(8,128)(2,1)S(1)}, bf16[1,64,2048]{2,1,0:T(8,128)(2,1)S(1)}, u32[]{:S(2)}, u32[]{:S(2)}) collective-permute-start(bf16[1,64,2048]{2,1,0:T(8,128)(2,1)S(1)} %dynamic-slice_convert_fusion.1), channel_id=1, source_target_pairs={{0,16},{8,24},{16,0},{24,8},{1,17},{9,25},{17,1},{25,9},{2,18},{10... | collective-permute-start | bytes 786440 | tf_op jit(solution)/shard_map/ppermute | solution.py:398
  (74 other events, 920.5 us)
Sparse Core Ops, SparseCore 0:
  46.8 88.0 all-gather.2
  138.4 76.0 all-gather.4

commit v2 on v1

--- a/solution.py
+++ b/solution.py
@@ -121,15 +121,13 @@
     )(core, tokens, *rows)
 
 
-def attention_kernel(
-    core, start, cos, sin, na_t, cot, wq, wk, wv, wo_near, wo_far, bq, bk, bv,
-    grads, merged, gq_out, gk_out, gv_out, sum_q, sum_k, sum_v,
-    bias, merged_t, gq_t, gk_t, gv_t, acc_k, acc_v,
-):
+def attention_kernel(core, start, cos, sin, na_t, cot, wq, wk, wv, wo, bq, bk, bv, *refs):
+    refs, scratch = refs[:-7], refs[-7:]
+    grads, merged, gq_out, gk_out, gv_out, sum_q, sum_k, sum_v = refs[-8:]
+    bias, merged_t, gq_t, gk_t, gv_t, acc_k, acc_v = scratch
     length = cot.shape[0]
-    step = pl.program_id(0)
-
-    @pl.when(step == 0)
+
+    @pl.when(pl.program_id(0) == 0)
     def _():
         key = lax.broadcasted_iota(jnp.int32, (length, length), 0)
         query = lax.broadcasted_iota(jnp.int32, (length, length), 1)
@@ -152,7 +150,7 @@
     q_t = rotate(project(wq, bq), 1.0).astype(bf16) * jnp.asarray(scale, bf16)
     k_t = rotate(project(wk, bk), 1.0).astype(bf16)
     v_t = project(wv, bv).astype(bf16)
-    gm_t = mul(by_core(core, wo_near[...], wo_far[...], 1), cot[...], 1, 1).astype(bf16)
+    gm_t = mul(wo[...], cot[...], 1, 1).astype(bf16)
     k, v = k_t.T, v_t.T
     for h in range(HEADS_STEP):
         hs = slice(h * HEAD_DIM, (h + 1) * HEAD_DIM)
@@ -177,39 +175,38 @@
     gq = rotate(gq_t[...], -1.0).astype(bf16)
     gk = rotate(gk_t[...], -1.0).astype(bf16)
     gv = gv_t[...].astype(bf16)
-    column = pl.multiple_of(lax.rem(step, 2) * WIDTH, WIDTH)
-    gq_out[...], gk_out[...], gv_out[...] = gq, gk, gv
-    merged[pl.ds(column, WIDTH), :] = merged_t[...]
+    merged[...], gq_out[...], gk_out[...], gv_out[...] = merged_t[...], gq, gk, gv
     for at, (part, out) in enumerate(((gq, sum_q), (gk, sum_k), (gv, sum_v))):
         out[...] = jnp.sum(part.astype(f32), axis=1, keepdims=True)
-        grads[:, pl.ds(at * HALF + column, WIDTH)] = mul(na_t[...], part, 1, 1).astype(bf16)
-
-
-def attention(core, last, start, cos, sin, na_t, cot, weights, near, far, bias_qkv):
+        grads[:, at * WIDTH : (at + 1) * WIDTH] = mul(na_t[...], part, 1, 1).astype(bf16)
+
+
+def attention(core, own, part, parts, start, cos, sin, na_t, cot, weights, bias_qkv, before=(), grads=None):
     length = cot.shape[0]
 
     def at(core, g):
-        return g + 2 * (core[0] if last else 1 - core[0])
-
-    def columns(part):
-        return pl.BlockSpec((D, WIDTH), lambda g, core: (0, 2 * part + g))
-
-    def entries(part):
-        return pl.BlockSpec((WIDTH, 1), lambda g, core: (4 * part + at(core, g), 0))
+        return part + g + 2 * (core[0] if own else 1 - core[0])
+
+    def columns(kind):
+        return pl.BlockSpec((D, WIDTH), lambda g, core: (0, 4 * kind + at(core, g)))
+
+    def entries(kind):
+        return pl.BlockSpec((WIDTH, 1), lambda g, core: (4 * kind + at(core, g), 0))
 
     sd = jax.ShapeDtypeStruct
-    rows_of_out = pl.BlockSpec((WIDTH, HALF), lambda g, core: (at(core, g), 3))
-    turned = pl.BlockSpec((WIDTH, length), lambda g, core: (g, 0))
-    summed = pl.BlockSpec((WIDTH, 1), lambda g, core: (g, 0))
-    args = (start, cos, sin, na_t, cot) + (weights,) * 3 + (near, far) + (bias_qkv,) * 3
+    args = (start, cos, sin, na_t, cot) + (weights,) * 4 + (bias_qkv,) * 3
     in_specs = [whole_block(a.shape) for a in args[:5]] + [columns(0), columns(1), columns(2)]
-    in_specs += [rows_of_out] * 2 + [entries(0), entries(1), entries(2)]
-    out_specs = [whole_block((D, 3 * HALF)), whole_block((HALF, length))]
-    out_specs += [turned] * 3 + [summed] * 3
-    out_shape = [sd((D, 3 * HALF), bf16)] + [sd((HALF, length), bf16)] * 4
-    out_shape += [sd((HALF, 1), f32)] * 3
+    in_specs += [pl.BlockSpec((WIDTH, D), lambda g, core: (at(core, g), 3))]
+    in_specs += [entries(0), entries(1), entries(2)]
+    out_specs = [pl.BlockSpec((D, 3 * WIDTH), lambda g, core: (0, part + g))]
+    out_specs += [pl.BlockSpec((WIDTH, length), lambda g, core: (at(core, g), 0))] * 4
+    out_specs += [entries(0)] * 3
+    out_shape = [sd((D, 4 * HALF), bf16)] + [sd((D, length), bf16)] * 4 + [sd((D, 1), f32)] * 3
+    kept = ((grads,) if grads is not None else ()) + tuple(before)
+    first = 1 + len(args)
     return call(
-        attention_kernel, (2,), in_specs, out_specs, out_shape, args,
+        attention_kernel, (parts,), in_specs, out_specs, out_shape, args, kept,
+        aliases={first + i: len(out_shape) - len(kept) + i for i in range(len(kept))},
         scratch=[
             pltpu.VMEM((length, length), f32),
             pltpu.VMEM((WIDTH, length), bf16),
@@ -219,60 +216,65 @@
             pltpu.VMEM((HEAD_DIM, length), f32),
             pltpu.VMEM((HEAD_DIM, length), f32),
         ],
-        flops=50 * 10**9, moved=2 * 10**7,
-    )(core, *args)
+        flops=parts * 25 * 10**9, moved=2 * 10**7,
+    )(core, *args, *kept)
+
+
+def grad_out_kernel(core, merged, cot, far, near):
+    grad = mul(merged[...], cot[...], 1, 0).astype(bf16)
+    left = core[0] == 0
+    far[...] = jnp.where(left, grad[:, HALF:], grad[:, :HALF])
+    near[...] = jnp.where(left, grad[:, :HALF], grad[:, HALF:])
+
+
+def grads_out(core, merged, cot, near):
+    args = (merged, cot)
+    rows = pl.BlockSpec((WIDTH, cot.shape[0]), lambda g, core: (g, 0))
+    return call(
+        grad_out_kernel, (D // WIDTH,), [rows, whole_block(cot.shape)],
+        [
+            pl.BlockSpec((WIDTH, HALF), lambda g, core: (g, 0)),
+            pl.BlockSpec((WIDTH, HALF), lambda g, core: (g, 3)),
+        ],
+        [jax.ShapeDtypeStruct((D, HALF), bf16), jax.ShapeDtypeStruct(near.shape, bf16)],
+        args, (near,), aliases={1 + len(args): 1}, flops=3 * 10**9, moved=10**7,
+    )(core, *args, near)
 
 
 def ffn_kernel(
-    core, nm, cot, w_in, w_down, b_in, merged_near, merged_far, *refs, which
+    core, nm, cot, w_in, wd_near, wd_far, b_in, far, near, active_out, grad_out, grad_b
 ):
-    far, near, active_out, grad_out, grad_b = refs[-5:]
+    w_down = by_core(core, wd_near[...], wd_far[...], 1)
     hidden = mul(nm[...], w_in[...], 1, 0) + b_in[...]
     cdf = 0.5 * (1.0 + lax.erf(hidden * (2.0**-0.5)))
     pdf = jnp.exp(-0.5 * hidden * hidden) * (1.0 / math.sqrt(2.0 * math.pi))
     active = (hidden * cdf).astype(bf16)
-    grad_hidden = (mul(cot[...], w_down[...], 1, 1) * (cdf + hidden * pdf)).astype(bf16)
+    grad_hidden = (mul(cot[...], w_down, 1, 1) * (cdf + hidden * pdf)).astype(bf16)
     active_out[...], grad_out[...] = active, grad_hidden
     grad_b[...] = jnp.sum(grad_hidden.astype(f32), axis=0, keepdims=True)
-    blocks = far.shape[0]
-    merged = jnp.where(core[0] == which, merged_near[...], merged_far[...])
-    grad_down = mul(active, cot[...], 0, 0).astype(bf16).reshape(blocks, -1, D)
-    grad_wo = mul(merged, cot[...], 1, 0).astype(bf16).reshape(blocks, -1, D)
-    at, left = grad_down.shape[1], core[0] == 0
-    for rows, grad in ((slice(0, at), grad_down), (slice(at, None), grad_wo)):
-        far[:, rows, :] = jnp.where(left, grad[..., HALF:], grad[..., :HALF])
-        near[:, rows, :] = jnp.where(left, grad[..., :HALF], grad[..., HALF:])
-
-
-def ffn_first(*refs):
-    ffn_kernel(*refs, which=0)
-
-
-def ffn_second(*refs):
-    ffn_kernel(*refs, which=1)
-
-
-def ffn(core, which, blocks, nm, cot, w_in, w_down, b_in, merged, after, before=()):
+    grad_down = mul(active, cot[...], 0, 0).astype(bf16)
+    left = core[0] == 0
+    far[...] = jnp.where(left, grad_down[:, HALF:], grad_down[:, :HALF]).reshape(far.shape)
+    near[...] = jnp.where(left, grad_down[:, :HALF], grad_down[:, HALF:]).reshape(near.shape)
+
+
+def ffn(core, blocks, nm, cot, w_in, wd_near, wd_far, b_in):
     length = nm.shape[0]
+    deep = FF // blocks
+    share = pl.BlockSpec((FF_TILE // deep, deep, HALF), lambda g, core: (g, 0, 0))
     sd = jax.ShapeDtypeStruct
-    steps = FF // FF_TILE // 2
-    share = (blocks // (2 * steps), (FF + D) // blocks, HALF)
-    columns = pl.BlockSpec((D, FF_TILE), lambda g, core: (0, steps * which + g))
-    tall = pl.BlockSpec((length, FF_TILE), lambda g, core: (0, steps * which + g))
-    row = pl.BlockSpec((1, FF_TILE), lambda g, core: (0, steps * which + g))
-    wide = pl.BlockSpec((FF_TILE, D), lambda g, core: (steps * which + g, 0))
-    heads = pl.BlockSpec((HALF // steps, length), lambda g, core: (g, 0))
-    grads = pl.BlockSpec(share, lambda g, core: (steps * which + g, 0, 0))
-    args = (nm, cot, w_in, w_down, b_in) + merged
-    more = tuple(before) + tuple(after)
+    columns = pl.BlockSpec((D, FF_TILE), lambda g, core: (0, g))
+    tall = pl.BlockSpec((length, FF_TILE), lambda g, core: (0, g))
+    row = pl.BlockSpec((1, FF_TILE), lambda g, core: (0, g))
+    half = pl.BlockSpec((FF_TILE, HALF), lambda g, core: (g, 0))
+    args = (nm, cot, w_in, wd_near, wd_far, b_in)
     return call(
-        ffn_second if which else ffn_first, (steps,),
-        [whole_block((length, D))] * 2 + [columns, wide, row, heads, heads],
-        [grads, grads, tall, tall, row],
-        [sd((blocks,) + share[1:], bf16)] * 2 + [sd((length, FF), bf16)] * 2 + [sd((1, FF), f32)],
-        args, more, aliases={1 + len(args) + at: at for at in range(len(before))},
-        flops=16 * 10**9, moved=3 * 10**7,
-    )(core, *args, *more)
+        ffn_kernel, (FF // FF_TILE,),
+        [whole_block((length, D))] * 2 + [columns, half, half, row],
+        [share, share, tall, tall, row],
+        [sd((blocks, 2 * deep, HALF), bf16)] * 2 + [sd((length, FF), bf16)] * 2 + [sd((1, FF), f32)],
+        args, flops=30 * 10**9, moved=5 * 10**7,
+    )(core, *args)
 
 
 def grad_in_kernel(core, nm_t, grad_hidden, far, near):
@@ -280,17 +282,20 @@
     half = pl.num_programs(0) // 2
 
     def store(ref):
-        ref[...] = mul(nm_t[...], grad_hidden[...], 1, 0).astype(bf16)
+        ref[...] = mul(nm_t[...], grad_hidden[...], 1, 0).astype(bf16).reshape(ref.shape)
 
     pl.when(step < half)(lambda: store(far))
     pl.when(step >= half)(lambda: store(near))
 
 
-def grads_in(core, nm_t, grad_hidden, after):
+def grads_in(core, nm_t, grad_hidden, far, near):
     length = nm_t.shape[1]
-    sd = jax.ShapeDtypeStruct
+    blocks = far.shape[0]
     half = FF // FF_TILE // 2
+    split = (blocks, 2 * half, D // blocks, FF_TILE)
     args = (nm_t, grad_hidden)
+    first = 1 + len(args)
+    cut = (blocks, 1, D // blocks, FF_TILE)
     return call(
         grad_in_kernel, (2 * half,),
         [
@@ -300,47 +305,47 @@
             ),
         ],
         [
-            pl.BlockSpec((D, FF_TILE), lambda g, core: (0, jnp.minimum(g, half - 1))),
-            pl.BlockSpec((D, FF_TILE), lambda g, core: (0, jnp.maximum(g - half, 0))),
+            pl.BlockSpec(cut, lambda g, core: (0, half + jnp.minimum(g, half - 1), 0, 0)),
+            pl.BlockSpec(cut, lambda g, core: (0, half + jnp.maximum(g - half, 0), 0, 0)),
         ],
-        [sd((D, FF // 2), bf16)] * 2, args, after, flops=9 * 10**9, moved=2 * 10**7,
-    )(core, *args, *after)
-
-
-def output_kernel(core, tokens, near_t, far_t, active, wo_near, wo_far, w_down, b_sum, output):
-    merged_t = by_core(core, near_t[...], far_t[...], 0)
-    att = by_core(core, mul(merged_t, wo_near[...], 0, 0), mul(merged_t, wo_far[...], 0, 0), 1)
-    fed = mul(active[...], w_down[...], 1, 0)
+        [jax.ShapeDtypeStruct(split, bf16)] * 2, args, (far.reshape(split), near.reshape(split)),
+        aliases={first: 0, first + 1: 1}, flops=9 * 10**9, moved=2 * 10**7,
+    )(core, *args, far.reshape(split), near.reshape(split))
+
+
+def output_kernel(core, tokens, merged, active, wo, wd_near, wd_far, b_sum, output):
+    att = mul(merged[...], wo[...], 0, 0)
+    fed = by_core(
+        core, mul(active[...], wd_near[...], 1, 0), mul(active[...], wd_far[...], 1, 0), 1
+    )
     output[...] = (tokens[...].astype(f32) + att + fed + b_sum[...]).astype(bf16)
 
 
-def outputs(core, tokens, near_t, far_t, active, near, far, w_down, b_sum, after):
+def outputs(core, tokens, merged, active, weights, wd_near, wd_far, b_sum, after):
     length = tokens.shape[0]
     tile = pl.BlockSpec((TOKEN_TILE, D), lambda g, core: (g, 0))
-    turned = pl.BlockSpec((HALF, TOKEN_TILE), lambda g, core: (0, g))
-    out_columns = pl.BlockSpec((D, HALF), lambda g, core: (0, 3), pipeline_mode=pl.Buffered(1))
-    args = (tokens, near_t, far_t, active, near, far, w_down, b_sum)
+    turned = pl.BlockSpec((D, TOKEN_TILE), lambda g, core: (0, g))
+    w_out = pl.BlockSpec((D, D), lambda g, core: (0, 3), pipeline_mode=pl.Buffered(1))
+    args = (tokens, merged, active, weights, wd_near, wd_far, b_sum)
     return call(
         output_kernel, (length // TOKEN_TILE,),
-        [tile, turned, turned, pl.BlockSpec((TOKEN_TILE, FF), lambda g, core: (g, 0))]
-        + [out_columns] * 2 + [whole_block((FF, D)), whole_block((1, D))],
+        [tile, turned, pl.BlockSpec((TOKEN_TILE, FF), lambda g, core: (g, 0)), w_out]
+        + [whole_block((FF, HALF))] * 2 + [whole_block((1, D))],
         [tile], [jax.ShapeDtypeStruct((length, D), bf16)], args, after,
         flops=11 * 10**9, moved=3 * 10**7,
     )(core, *args, *after)[0]
 
 
 def input_kernel(
-    core, tokens, cot, gq_near, gk_near, gv_near, gq_far, gk_far, gv_far, grad_hidden,
-    near, far, w_in, gain_one, gain_two, input_grad, sums,
+    core, tokens, cot, gq, gk, gv, grad_hidden, w_qkv, w_in, gain_one, gain_two, input_grad, sums
 ):
     inputs = tokens[...].astype(f32)
     centre = inputs - jnp.mean(inputs, axis=-1, keepdims=True)
     spread = jnp.mean(centre * centre, axis=-1, keepdims=True)
     rstd = lax.rsqrt(spread + norm_eps)
     normed = centre * rstd
-    joined_near = jnp.concatenate([gq_near[...], gk_near[...], gv_near[...]], axis=0)
-    joined_far = jnp.concatenate([gq_far[...], gk_far[...], gv_far[...]], axis=0)
-    grad_na = mul(joined_near, near[...], 0, 1) + mul(joined_far, far[...], 0, 1)
+    joined = jnp.concatenate([gq[...], gk[...], gv[...]], axis=0)
+    grad_na = mul(joined, w_qkv[...], 0, 1)
     grad_nm = mul(grad_hidden[...], w_in[...], 1, 1)
     grad_normed = grad_na * gain_one[...] + grad_nm * gain_two[...]
     cotangent = cot[...].astype(f32)
@@ -358,17 +363,18 @@
         sums[at : at + 1, :] += jnp.sum(terms, axis=0, keepdims=True)
 
 
-def input_grads(core, tokens, cot, joined, grad_hidden, near, far, w_in, gains, after):
+def input_grads(core, tokens, cot, joined, grad_hidden, weights, w_in, gains, after):
     length = tokens.shape[0]
     tile = pl.BlockSpec((TOKEN_TILE, D), lambda g, core: (g, 0))
-    turned = pl.BlockSpec((HALF, TOKEN_TILE), lambda g, core: (0, g))
-    share = pl.BlockSpec((D, 3 * HALF), lambda g, core: (0, 0), pipeline_mode=pl.Buffered(1))
-    args = (tokens, cot) + joined + (grad_hidden, near, far, w_in) + gains
+    turned = pl.BlockSpec((D, TOKEN_TILE), lambda g, core: (0, g))
+    once = functools.partial(pl.BlockSpec, pipeline_mode=pl.Buffered(1))
+    args = (tokens, cot) + joined + (grad_hidden, weights, w_in) + gains
     sd = jax.ShapeDtypeStruct
     return call(
         input_kernel, (length // TOKEN_TILE,),
-        [tile, tile] + [turned] * 6 + [pl.BlockSpec((TOKEN_TILE, FF), lambda g, core: (g, 0))]
-        + [share] * 2 + [whole_block((D, FF))] + [whole_block((1, D))] * 2,
+        [tile, tile] + [turned] * 3 + [pl.BlockSpec((TOKEN_TILE, FF), lambda g, core: (g, 0))]
+        + [once((D, 3 * D), lambda g, core: (0, 0)), once((D, FF), lambda g, core: (0, 0))]
+        + [whole_block((1, D))] * 2,
         [tile, whole_block((8, D))],
         [sd((length, D), f32), sd((8, D), f32)], args, after, flops=15 * 10**9, moved=4 * 10**7,
     )(core, *args, *after)
@@ -436,15 +442,10 @@
             whole = lax.dynamic_update_slice(whole, part, (0,) + at + (0, 0))
         return whole.reshape(-1, value.shape[-1])
 
-    def owners(self, held, core, parts=1):
-        cuts = [held.shape[0] * 4 // 5] if parts == 2 else []
-        mine, other = [], []
-        for part in jnp.split(held, cuts):
-            rows = part.shape[0] // 2
-            mine.append(lax.dynamic_slice_in_dim(part, core * rows, rows))
-            other.append(lax.dynamic_slice_in_dim(part, (1 - core) * rows, rows))
-        mine = jnp.concatenate(mine)
-        came = self.swap("c", jnp.concatenate(other))
+    def owners(self, held, core):
+        rows = held.shape[0] // 2
+        mine = lax.dynamic_slice_in_dim(held, core * rows, rows)
+        came = self.swap("c", lax.dynamic_slice_in_dim(held, (1 - core) * rows, rows))
         return jnp.concatenate(
             [jnp.where(core == 0, mine, came), jnp.where(core == 0, came, mine)], axis=1
         )
@@ -461,13 +462,13 @@
         )
 
     def term(self, odd, y=None, x=None):
+        _, _, _, _, rows, n = self.near.shape
+        size = (self.links.nz // 2, 1, 1 if y is not None else 2, 1 if x is not None else 2, rows, n)
+        start = (0, odd, 0 if y is None else y, 0 if x is None else x, 0, 0)
+        shape = tuple(count for at, count in enumerate(size) if at in (0, 4, 5) or count == 2)
+
         def cut(v):
-            v = v[:, odd]
-            if x is not None:
-                v = lax.dynamic_index_in_dim(v, x, 2, False)
-            if y is not None:
-                v = lax.dynamic_index_in_dim(v, y, 1, False)
-            return v.astype(f32)
+            return lax.dynamic_slice(v, start, size).reshape(shape).astype(f32)
 
         return cut(self.near) + cut(self.came)
 
@@ -492,15 +493,21 @@
         low = self.z % 2 == 0
         self.keep, self.send = jnp.where(low, even, odd), jnp.where(low, odd, even).astype(bf16)
 
-    def finish(self, *after):
-        came = later(self.links.swap("z", self.send), *after) if after else self.links.swap("z", self.send)
-        held = self.keep + came.astype(f32)
-        for bit in self.links.bits("z")[:-1][::-1]:
-            mine = self.z // (2 * bit) % 2
-            send = lax.dynamic_slice_in_dim(held, (1 - mine) * bit, bit).astype(bf16)
-            keep = lax.dynamic_slice_in_dim(held, mine * bit, bit)
-            held = keep + self.links.swap("z", send, 2 * bit).astype(f32)
-        return held[0]
+        self.bits = [1] + [2 * bit for bit in self.links.bits("z")[:-1]][::-1]
+
+    def advance(self, *after):
+        came = self.links.swap("z", self.send, self.bits.pop(0))
+        self.held = self.keep + (later(came, *after) if after else came).astype(f32)
+        if self.bits:
+            bit = self.bits[0]
+            mine, size = self.z // bit % 2, bit // 2
+            self.send = lax.dynamic_slice_in_dim(self.held, (1 - mine) * size, size).astype(bf16)
+            self.keep = lax.dynamic_slice_in_dim(self.held, mine * size, size)
+
+    def finish(self):
+        while self.bits:
+            self.advance()
+        return self.held[0]
 
 
 def per_device(
@@ -531,21 +538,22 @@
     rows = w_qkv.shape[0]
     per_row = vectors.shape[0] // rows
 
-    spare = jnp.pad(vectors.astype(bf16).reshape(rows, per_row), ((0, 0), (0, 128 - per_row)))
-    halves = jnp.concatenate([w_qkv, w_out], axis=1).astype(bf16).reshape(rows, 4, 2, HALF)
-
-    def share(at):
-        part = lax.dynamic_index_in_dim(halves, at, 2, False).reshape(rows, 4 * HALF)
-        return jnp.concatenate([part, spare], axis=1)
-
-    mine, came = share(core), links.swap("c", share(1 - core))
-    near = links.gather(
+    spare = jnp.pad(vectors.reshape(rows, per_row), ((0, 0), (0, 128 - per_row)))
+    w_in_all = lax.all_gather(
+        jnp.concatenate([w_in, spare], axis=1).astype(bf16), every, axis=0, tiled=True
+    )
+    halves = w_down.astype(bf16).reshape(-1, 2, HALF)
+    mine = lax.dynamic_index_in_dim(halves, core, 1, False)
+    came = links.swap("c", lax.dynamic_index_in_dim(halves, 1 - core, 1, False))
+    wd_near = links.gather(
         jnp.where(core == 0, jnp.concatenate([mine, came]), jnp.concatenate([came, mine]))
     )
-    far = links.swap("c", near)
-    w_in_all = lax.all_gather(rounded(core_ref, w_in, (links.column,)), every, axis=0, tiled=True)
-    w_down_all = lax.all_gather(rounded(core_ref, w_down, (links.column,)), every, axis=0, tiled=True)
-    vector_all = near[:, 4 * HALF : 4 * HALF + per_row].reshape(-1).astype(f32)
+    wd_far = links.swap("c", wd_near)
+    weights = lax.all_gather(
+        rounded(core_ref, jnp.concatenate([w_qkv, w_out], axis=1), (links.column,)),
+        every, axis=0, tiled=True,
+    )
+    vector_all = w_in_all[:, FF : FF + per_row].reshape(-1).astype(f32)
     b_qkv, b_out, b_in, b_down, gain_one, shift_one, gain_two, shift_two = split_vector(vector_all)
 
     positions = positions_of(doc_ids)
@@ -556,59 +564,70 @@
     na, nm, na_t, nm_t = norms(
         core_ref, tokens, (gains[0], shift_one.reshape(1, D), gains[1], shift_two.reshape(1, D))
     )
-    common = (start, jnp.cos(angles), jnp.sin(angles), na_t, cotangent)
+    cos, sin = jnp.cos(angles), jnp.sin(angles)
     bias_qkv = b_qkv.reshape(3 * D, 1)
-    grads_far, merged_far, *joined_far = attention(
-        core_ref, False, *common, far, near, far, bias_qkv
-    )
-    came_heads = links.swap("c", grads_far)
-    grads_near, merged_near, *joined_near = attention(
-        core_ref, True, *common, near, near, far, bias_qkv
-    )
-    heads = Scatter(links, grads_near, came_heads)
     blocks = D // rows // 2
-    fixed = (nm, cotangent, w_in_all, w_down_all, b_in.reshape(1, FF), (merged_near, merged_far))
-    filled = ffn(core_ref, 0, blocks, *fixed, heads.first)
-    heads.step_one(filled[4])
-    down_far, down_near, active, grad_hidden, sum_in = ffn(
-        core_ref, 1, blocks, *fixed, heads.second, filled
-    )
-    came_down = links.swap("c", down_far)
-    heads.step_two(sum_in)
-    in_far, in_near = grads_in(core_ref, nm_t, grad_hidden, (heads.send,))
-    came_in = links.swap("c", in_far)
-    down = Scatter(links, down_near, came_down)
+    far, near, active, grad_hidden, sum_in = ffn(
+        core_ref, blocks, nm, cotangent, w_in_all, wd_near, wd_far, b_in.reshape(1, FF)
+    )
+    far, near = grads_in(core_ref, nm_t, grad_hidden, far, near)
+    deep = 2 * FF // blocks
+    hidden = Scatter(
+        links, near.reshape(blocks * deep, HALF), links.swap("c", far).reshape(blocks * deep, HALF)
+    )
+    heads = functools.partial(attention, core_ref)
+
+    def common(*after):
+        return (later(start, *after), cos, sin, na_t, cotangent, weights, bias_qkv)
+
+    far, *kept = heads(False, 0, 2, *common(*hidden.first))
+    came_heads = links.swap("c", far)
+    hidden.step_one(kept[4])
+    near, *kept = heads(True, 0, 1, *common(*hidden.second), kept)
+    hidden.step_two(kept[4])
+    near, *kept = heads(True, 1, 1, *common(hidden.send), kept, near)
+    merged, *joined = kept[:4]
+    hidden.advance(kept[4])
+    out_far, near = grads_out(core_ref, merged, later(cotangent, hidden.send), near)
+    came_out = links.swap("c", out_far)
+    last = Scatter(
+        links, near, lax.dynamic_update_slice(came_heads, came_out, (0, 3 * HALF))
+    )
     output = outputs(
-        core_ref, tokens, merged_near, merged_far, active, near, far, w_down_all,
-        (b_out + b_down).reshape(1, D), down.first,
-    )
-    grad_heads = links.owners(heads.finish(output[:8, :128]), core)
-    inner = Scatter(links, in_near, came_in)
-    down.step_one(output[:8, :128])
+        core_ref, later(tokens, *last.first, hidden.send), merged, active, weights, wd_near, wd_far,
+        (b_out + b_down).reshape(1, D), (),
+    )
+    last.step_one(output)
     input_grad, sums = input_grads(
-        core_ref, tokens, cotangent, tuple(joined_near[:3] + joined_far[:3]), grad_hidden,
-        near, far, w_in_all, gains, down.second + inner.first + (output,),
-    )
-    heads_sums = [
-        part[:, 0]
-        for mine, other in zip(joined_near[3:], joined_far[3:])
-        for part in (jnp.where(core == 0, mine, other), jnp.where(core == 0, other, mine))
-    ]
+        core_ref, later(tokens, *last.second), cotangent, tuple(joined), grad_hidden, weights, w_in_all,
+        gains, (output,),
+    )
+    hidden.advance(output)
+    held = hidden.finish()
+    deep = deep // 2
+    held = jnp.concatenate(
+        [
+            held[:deep].reshape(2, deep // 2, HALF),
+            held[deep:].reshape(-1, 2, rows, HALF).transpose(1, 0, 2, 3).reshape(2, -1, HALF),
+        ],
+        axis=1,
+    ).reshape(-1, HALF)
+    grad_rows = links.owners(held, core)
+    grad_down = grad_rows[: deep // 2]
+    grad_in = grad_rows[deep // 2 :].reshape(-1, rows, 2, HALF).transpose(1, 2, 0, 3).reshape(rows, FF)
+    last.step_two(sums)
     vector_terms = jnp.concatenate(
-        heads_sums + [sums[0], sum_in[0], sums[0], sums[1], sums[2], sums[3], sums[4]]
+        [part[:, 0] for part in kept[4:]] + [sums[0], sum_in[0], sums[0], sums[1], sums[2], sums[3], sums[4]]
     )
     vector_total = links.total(vector_terms.reshape(-1, 128)).reshape(-1)
     count_own = vectors.shape[0]
     grad_vectors = lax.dynamic_slice_in_dim(
         vector_total, lax.axis_index(every) * count_own, count_own
     )
-    grad_qkv = grad_heads.reshape(rows, 2, 3, HALF).transpose(0, 2, 1, 3).reshape(rows, 3 * D)
-    down.step_two(sums)
-    inner.step_one(sums)
-    grad_rows = links.owners(down.finish(), core, 2)
-    grad_down, grad_out = grad_rows[: 4 * rows], grad_rows[4 * rows :]
-    inner.step_two()
-    grad_in = links.owners(inner.finish(), core)
+    grad_heads = links.owners(last.finish(), core).reshape(rows, 2, 4 * HALF)
+    grad_out = grad_heads[:, :, 3 * HALF :].reshape(rows, D)
+    grad_qkv = grad_heads[:, :, : 3 * HALF].reshape(rows, 2, 2, 3, WIDTH)
+    grad_qkv = grad_qkv.transpose(0, 3, 1, 2, 4).reshape(rows, 3 * D)
     pieces = (grad_qkv, grad_out, grad_in, grad_down, grad_vectors)
     local_square = sum(jnp.sum(piece * piece) for piece in pieces)
     norm = jnp.sqrt(links.total(jnp.broadcast_to(local_square, (8, 128)))[0, 0])

time: 546 us -> 493 us (0.903)
  waiting for transfers between devices: 149 us -> 125 us
  local copies, waits for them, and re-layouts: 46.4 us -> 22.7 us
  starting transfers between devices: 45.5 us -> 36 us
    ppermute x42 -> x35, waiting for transfers between devices: 149 us -> 119 us  [swap(): lax.ppermute(value, axis, [(i, i ^ bit) for i in range(self.sizes[axis])])]
    slice x7 -> x4, local copies, waits for them, and re-layouts: 18.1 us -> 0.26 us  [the longest x2 0.11 us: per_device(): grad_qkv = grad_heads[:, :, :3 * HALF].reshape(rows, 2, 2, 3, WIDTH)]
    ppermute x42 -> x35, starting transfers between devices: 45.4 us -> 35.9 us  [swap(): lax.ppermute(value, axis, [(i, i ^ bit) for i in range(self.sizes[axis])])]
    convert_element_type x10 -> x3, local copies, waits for them, and re-layouts: 9.42 us -> 0.46 us  [the longest x1 0.36 us: per_device(): vector_all = w_in_all[:, FF:FF + per_row].reshape(-1).astype(f32)]
    all_gather x2, waiting for transfers between devices: 0.01 us -> 5.89 us  [the longest x1 5.89 us: per_device(): lax.all_gather(jnp.concatenate([w_in, spare], axis=1).astype(bf16), every...]
    convert_element_type x5 -> x2, other arithmetic: 7.56 us -> 2.06 us  [the longest x1 1.07 us: per_device(): halves = w_down.astype(bf16).reshape(-1, 2, HALF)]
    pallas_call x6 -> x7, Pallas kernels: 202 us -> 205 us  [the longest x3 115 us: attention(): call(attention_kernel, (parts,), in_specs, out_specs, out_shape, args, ke...]
  transfers between devices with their start and end apart: 44 -> 37, of which waited for: 20 -> 20; matrix products, arithmetic and copies ran while one was open for 15% -> 14% of each run, Pallas kernels for 39% -> 46%
where the time goes in v2:
time: 493 us; the launch traced here: 490 us
  Pallas kernels  227 us (46%)
  waiting for transfers between devices  125 us (25%)
  other arithmetic  58.6 us (12%)
  starting transfers between devices  36 us (7%)
  local copies, waits for them, and re-layouts  22.7 us (5%)
  between operations  20.2 us (4%)
    ppermute x35, waiting for transfers between devices, swap(): lax.ppermute(value, axis, [(i, i ^ bit) for i in range(self.sizes[axis])])  119 us
    pallas_call x3, Pallas kernels, attention(): call(attention_kernel, (parts,), in_specs, out_specs, out_shape, args, ke...  115 us
    pallas_call x1, Pallas kernels, ffn(): call(ffn_kernel, (FF // FF_TILE,), [whole_block((length, D))] * 2 + [colu...  38.2 us
    ppermute x35, starting transfers between devices, swap(): lax.ppermute(value, axis, [(i, i ^ bit) for i in range(self.sizes[axis])])  35.9 us
    pallas_call x1, Pallas kernels, input_grads(): call(input_kernel, (length // TOKEN_TILE,), [tile, tile] + [turned] * 3 +...  27.5 us
    pallas_call x1, Pallas kernels, outputs(): call(output_kernel, (length // TOKEN_TILE,), [tile, turned, pl.BlockSpec(...  18 us
    pallas_call x1, Pallas kernels, grads_in(): call(grad_in_kernel, (2 * half,), [whole_block((D, length)), pl.BlockSpec...  14.6 us
  transfers between devices with their start and end apart: 37, of which 20 were waited for; matrix products, arithmetic and copies ran while one was open for 14% of the time, Pallas kernels for 46%

profile of v2, /device:TPU:0, one launch (start us, length us, event | category | flops | bytes accessed | tf_op | source)
XLA Modules:
  0.0 489.9 jit_solution(8079681176576513735)
XLA Ops:
  13.3 4.0 collective-permute-start.1
  17.4 16.1 %collective-permute-done.1 = bf16[1,256,512]{2,1,0:T(8,128)(2,1)S(1)} collective-permute-done((bf16[1,256,512]{2,1,0:T(8,128)(2,1)S(1)}, bf16[1,256,512]{2,1,0:T(8,128)(2,1)S(1)}, u32[]{:S(2)}, u32[]{:S(2)}) %collective-permute-start.1) | collective-permute-done | bytes 262176 | tf_op jit(solution)/shard_map/ppermute | solution.py:404
  35.9 17.5 %collective-permute-done.2.refs_2_ = bf16[2,256,512]{2,1,0:T(8,128)(2,1)S(1)} collective-permute-done((bf16[2,256,512]{2,1,0:T(8,128)(2,1)S(1)}, bf16[2,256,512]{2,1,0:T(8,128)(2,1)S(1)}, u32[]{:S(2)}, u32[]{:S(2)}) %collective-permute-start.2) | collective-permute-done | bytes 524320 | tf_op jit(solution)/shard_map/ppermute | solution.py:404
  56.7 8.3 %collective-permute-done.3 = bf16[2,1,1,1,256,512]{5,4,0,3,2,1:T(8,128)(2,1)S(1)} collective-permute-done((bf16[2,1,1,1,256,512]{5,4,0,3,2,1:T(8,128)(2,1)S(1)}, bf16[2,1,1,1,256,512]{5,4,0,3,2,1:T(8,128)(2,1)S(1)}, u32[]{:S(2)}, u32[]{:S(2)}) %collective-permute-start.3) | collective-permute-done | bytes 524320 | tf_op jit(solution)/shard_map/ppermute | solution.py:404
  74.0 30.1 %collective-permute-done.4 = bf16[2,1,2,1,256,512]{5,4,0,3,2,1:T(8,128)(2,1)} collective-permute-done((bf16[2,1,2,1,256,512]{5,4,0,3,2,1:T(8,128)(2,1)}, bf16[2,1,2,1,256,512]{5,4,0,3,2,1:T(8,128)(2,1)}, u32[]{:S(2)}, u32[]{:S(2)}) %collective-permute-start.4) | collective-permute-done | bytes 1048608 | tf_op jit(solution)/shard_map/ppermute | solution.py:404
  112.7 5.9 %all-gather.3.cloned.1.call-done.refs_3_.refs_8_ = bf16[1024,4224]{1,0:T(8,128)(2,1)} async-done(((bf16[32,4224]{1,0:T(8,128)(2,1)}), bf16[1024,4224]{1,0:T(8,128)(2,1)}) %all-gather.3.cloned.1.call-update) | async-done | bytes 8650768 | tf_op jit(solution)/shard_map/all_gather | solution.py:542
  121.2 6.0 %norm_kernel.1 = (bf16[1024,1024]{1,0:T(8,128)(2,1)}, bf16[1024,1024]{1,0:T(8,128)(2,1)}, bf16[1024,1024]{1,0:T(8,128)(2,1)}, bf16[1024,1024]{1,0:T(8,128)(2,1)}) custom-call(s32[1]{0:T(128)} %bitcast.refs_0_, bf16[1024,1024]{1,0:T(8,128)(2,1)} %refs_1_.3, f32[1,1024]{1,0:T(1,128)} %bitcast.218, f32[1,1024]{1,0:T(1,128)} %bitcast.221, f32[1,1024]{1,0:T(1,128)} %bitcast.216, ...), custom_call_target="tpu_custom_call" | custom-call | flops 10000000 | bytes 10000000 | tf_op jit(solution)/shard_map/norm_kernel/pallas_call | solution.py:116
  127.1 38.2 %ffn_kernel.1 = (bf16[16,512,512]{2,1,0:T(8,128)(2,1)}, bf16[16,512,512]{2,1,0:T(8,128)(2,1)}, bf16[1024,4096]{1,0:T(8,128)(2,1)}, bf16[1024,4096]{1,0:T(8,128)(2,1)}, f32[1,4096]{1,0:T(1,128)}) custom-call(s32[1]{0:T(128)} %bitcast.refs_0_, bf16[1024,1024]{1,0:T(8,128)(2,1)} %get-tuple-element.78.refs_1_, bf16[1024,1024]{1,0:T(8,128)(2,1)} %refs_2_.4, ...), custom_call_target="tpu_custom_call" | custom-call | flops 30000001024 | bytes 50000000 | tf_op jit(solution)/shard_map/ffn_kernel/pallas_call | solution.py:271
  165.4 14.6 %grad_in_kernel.1 = (bf16[16,8,64,512]{3,2,1,0:T(8,128)(2,1)}, bf16[16,8,64,512]{3,2,1,0:T(8,128)(2,1)}) custom-call(s32[1]{0:T(128)} %bitcast.refs_0_, bf16[1024,1024]{1,0:T(8,128)(2,1)} %get-tuple-element.77.refs_1_, bf16[1024,4096]{1,0:T(8,128)(2,1)} %get-tuple-element.79.refs_2_.refs_6_, ...), custom_call_target="tpu_custom_call", output_to_operand_aliasing={{0}: (3, {}), {1}: (4, {})} | custom-call | flops 8999999488 | bytes 20000000 | tf_op jit(solution)/shard_map/grad_in_kernel/pallas_call | solution.py:299
  184.0 10.2 %collective-permute-done.8 = bf16[16,8,64,512]{3,2,1,0:T(8,128)(2,1)} collective-permute-done((bf16[16,8,64,512]{3,2,1,0:T(8,128)(2,1)}, bf16[16,8,64,512]{3,2,1,0:T(8,128)(2,1)}, u32[]{:S(2)}, u32[]{:S(2)}) %collective-permute-start.8) | collective-permute-done | bytes 8388640 | tf_op jit(solution)/shard_map/ppermute | solution.py:404
  194.3 4.4 fusion
  198.7 4.2 fusion.1
  205.0 62.1 %attention_kernel.3 = (bf16[1024,2048]{1,0:T(8,128)(2,1)}, bf16[1024,1024]{1,0:T(8,128)(2,1)}, bf16[1024,1024]{1,0:T(8,128)(2,1)}, bf16[1024,1024]{1,0:T(8,128)(...) custom-call(s32[1]{0:T(128)} %bitcast.refs_0_, ...), custom_call_target="tpu_custom_call" | custom-call | flops 49999998976 | bytes 20000000 | tf_op jit(solution)/shard_map/attention_kernel/pallas_call | solution.py:207
  267.2 4.3 fusion.3
  273.5 26.1 %attention_kernel.4 = (bf16[1024,2048]{1,0:T(8,128)(2,1)}, bf16[1024,1024]{1,0:T(8,128)(2,1)}, bf16[1024,1024]{1,0:T(8,128)(2,1)}, bf16[1024,1024]{1,0:T(8,128)(...) custom-call(s32[1]{0:T(128)} %bitcast.refs_0_, ...), custom_call_target="tpu_custom_call", output_to_operand_aliasing={{1}: (13, {}), {2}: (14, {}), {3}: (15, {}), {4}: (16, {}),... | custom-call | flops 24999999488 | bytes 20000000 | tf_op jit(solution)/shard_map/attention_kernel/pallas_call | solution.py:207
  299.6 4.6 select_convert_fusion
  304.1 26.6 %attention_kernel.5 = (bf16[1024,2048]{1,0:T(8,128)(2,1)}, bf16[1024,1024]{1,0:T(8,128)(2,1)}, bf16[1024,1024]{1,0:T(8,128)(2,1)}, bf16[1024,1024]{1,0:T(8,128)(...) custom-call(s32[1]{0:T(128)} %bitcast.refs_0_, ...), custom_call_target="tpu_custom_call", output_to_operand_aliasing={{0}: (13, {}), {1}: (14, {}), {2}: (15, {}), {3}: (16, {}),... | custom-call | flops 24999999488 | bytes 20000000 | tf_op jit(solution)/shard_map/attention_kernel/pallas_call | solution.py:207
  335.8 6.1 %grad_out_kernel.1 = (bf16[1024,512]{1,0:T(8,128)(2,1)}, bf16[1024,2048]{1,0:T(8,128)(2,1)}) custom-call(s32[1]{0:T(128)} %bitcast.refs_0_, bf16[1024,1024]{1,0:T(8,128)(2,1)} %get-tuple-element.107.refs_1_.refs_2_, bf16[1024,1024]{1,0:T(8,128)(2,1)} %refs_2_.4, bf16[1024,2048]{1,0:T(8,128)(2,1)} %get-tuple-element.111.refs_3_), custom_call_target="tpu_custom_call", output_to_operand_aliasing={{1}: (3, {})} | custom-call | flops 3000000000 | bytes 10000000 | tf_op jit(solution)/shard_map/grad_out_kernel/pallas_call | solution.py:233
  342.6 4.5 collective-permute-start.23
  357.0 18.0 %output_kernel.1.refs_11_ = bf16[1024,1024]{1,0:T(8,128)(2,1)} custom-call(s32[1]{0:T(128)} %bitcast.refs_0_, bf16[1024,1024]{1,0:T(8,128)(2,1)} %refs_1_.3, bf16[1024,1024]{1,0:T(8,128)(2,1)} %get-tuple-element.107.refs_1_.refs_2_, bf16[1024,4096]{1,0:T(8,128)(2,1)} %get-tuple-element.116.refs_3_, ...), custom_call_target="tpu_custom_call" | custom-call | flops 11000000512 | bytes 30000000 | tf_op jit(solution)/shard_map/output_kernel/pallas_call | solution.py:330
  385.9 27.5 %input_kernel.1 = (f32[1024,1024]{1,0:T(8,128)}, f32[8,1024]{1,0:T(8,128)}) custom-call(s32[1]{0:T(128)} %bitcast.refs_0_, bf16[1024,1024]{1,0:T(8,128)(2,1)} %refs_1_.3, bf16[1024,1024]{1,0:T(8,128)(2,1)} %refs_2_.4, bf16[1024,1024]{1,0:T(8,128)(2,1)} %get-tuple-element.120.refs_3_, bf16[1024,1024]{1,0:T(8,128)(2,1)} %get-tuple-element.121.refs_4_, ...), custom_call_target="tpu_custom_call" | custom-call | flops 15000000512 | bytes 40000000 | tf_op jit(solution)/shard_map/input_kernel/pallas_call | solution.py:373
  423.1 8.2 %collective-permute-done.20 = bf16[2,64,2048]{2,1,0:T(8,128)(2,1)S(1)} collective-permute-done((bf16[2,64,2048]{2,1,0:T(8,128)(2,1)S(1)}, bf16[2,64,2048]{2,1,0:T(8,128)(2,1)S(1)}, u32[]{:S(2)}, u32[]{:S(2)}) %collective-permute-start.20) | collective-permute-done | bytes 524320 | tf_op jit(solution)/shard_map/ppermute | solution.py:404
  438.6 3.9 collective-permute-done.28
  444.7 5.0 %collective-permute-done.21 = bf16[1,64,2048]{2,1,0:T(8,128)(2,1)S(1)} collective-permute-done((bf16[1,64,2048]{2,1,0:T(8,128)(2,1)S(1)}, bf16[1,64,2048]{2,1,0:T(8,128)(2,1)S(1)}, u32[]{:S(2)}, u32[]{:S(2)}) %collective-permute-start.21) | collective-permute-done | bytes 262176 | tf_op jit(solution)/shard_map/ppermute | solution.py:404
  (227 shorter events, 113.3 us)
Async XLA Ops:
  7.2 111.4 %all-gather.3.cloned.1.call-start = ((), (), s32[]{:S(2)}) async-start(), calls=%async_computation | async-start | bytes 8921088 | tf_op jit(solution)/shard_map/all_gather | solution.py:542
  9.9 195.1 %all-gather.5.cloned.1.call-start = ((), (), s32[]{:S(2)}) async-start(), calls=%async_computation.1 | async-start | bytes 8650752 | tf_op jit(solution)/shard_map/all_gather | solution.py:552
  13.3 20.1 %collective-permute-start.1 = (bf16[1,256,512]{2,1,0:T(8,128)(2,1)S(1)}, bf16[1,256,512]{2,1,0:T(8,128)(2,1)S(1)}, u32[]{:S(2)}, u32[]{:S(2)}) collective-permute-start(bf16[1,256,512]{2,1,0:T(8,128)(2,1)S(1)} %maximum_select_fusion.3), channel_id=1, source_target_pairs={{0,16},{8,24},{16,0},{24,8},{1,17},{9,25},{17,1},{25,9},{2,18},{10... | collective-permute-start | bytes 786440 | tf_op jit(solution)/shard_map/ppermute | solution.py:404
  33.5 19.9 %collective-permute-start.2 = (bf16[2,256,512]{2,1,0:T(8,128)(2,1)S(1)}, bf16[2,256,512]{2,1,0:T(8,128)(2,1)S(1)}, u32[]{:S(2)}, u32[]{:S(2)}) collective-permute-start(bf16[2,256,512]{2,1,0:T(8,128)(2,1)S(1)} %maximum_select_fusion.2), channel_id=1, source_target_pairs={{0,8},{8,0},{16,24},{24,16},{1,9},{9,1},{17,25},{25,17},{2,10},{10... | collective-permute-start | bytes 1572872 | tf_op jit(solution)/shard_map/ppermute | solution.py:404
  55.0 12.5 %collective-permute-start.5 = (bf16[2,1,1,1,256,512]{5,4,0,3,2,1:T(8,128)(2,1)S(1)}, bf16[2,1,1,1,256,512]{5,4,0,3,2,1:T(8,128)(2,1)S(1)}, u32[]{:S(2)}, u32[]{:S(2)}) collective-permute-start(bf16[2,1,1,1,256,512]{5,4,0,3,2,1:T(8,128)(2,1)S(1)} %get-tuple-element.161), channel_id=1, source_target_pairs={{0,2},{2,0},{1,3},{3,1},{4,6},{6,4},{5,7},{7,5},{8,10},{10,8},{9,1... | collective-permute-start | bytes 1572872 | tf_op jit(solution)/shard_map/ppermute | solution.py:404
  66.2 37.9 %collective-permute-start.4 = (bf16[2,1,2,1,256,512]{5,4,0,3,2,1:T(8,128)(2,1)}, bf16[2,1,2,1,256,512]{5,4,0,3,2,1:T(8,128)(2,1)}, u32[]{:S(2)}, u32[]{:S(2)}) collective-permute-start(bf16[2,1,2,1,256,512]{5,4,0,3,2,1:T(8,128)(2,1)} %maximum_select_fusion), channel_id=1, source_target_pairs={{0,2},{2,0},{1,3},{3,1},{4,6},{6,4},{5,7},{7,5},{8,10},{10,8},{9,1... | collective-permute-start | bytes 3145736 | tf_op jit(solution)/shard_map/ppermute | solution.py:404
  68.6 39.0 %collective-permute-start.6 = (bf16[2,1,1,2,256,512]{5,4,0,3,2,1:T(8,128)(2,1)}, bf16[2,1,1,2,256,512]{5,4,0,3,2,1:T(8,128)(2,1)}, u32[]{:S(2)}, u32[]{:S(2)}) collective-permute-start(bf16[2,1,1,2,256,512]{5,4,0,3,2,1:T(8,128)(2,1)} %maximum_select_fusion.1), channel_id=1, source_target_pairs={{0,4},{4,0},{1,5},{5,1},{2,6},{6,2},{3,7},{7,3},{8,12},{12,8},{9,1... | collective-permute-start | bytes 3145736 | tf_op jit(solution)/shard_map/ppermute | solution.py:404
  110.1 17.1 %collective-permute-start.7 = (bf16[4096,512]{1,0:T(8,128)(2,1)}, bf16[4096,512]{1,0:T(8,128)(2,1)}, u32[]{:S(2)}, u32[]{:S(2)}) collective-permute-start(bf16[4096,512]{1,0:T(8,128)(2,1)} %bitcast.12.refs_4_.refs_5_), channel_id=1, source_target_pairs={{0,1},{1,0},{2,3},{3,2},{4,5},{5,4},{6,7},{7,6},{8,9},{9,8},{10,11... | collective-permute-start | bytes 12582920 | tf_op jit(solution)/shard_map/ppermute | solution.py:404
  179.9 14.3 %collective-permute-start.8 = (bf16[16,8,64,512]{3,2,1,0:T(8,128)(2,1)}, bf16[16,8,64,512]{3,2,1,0:T(8,128)(2,1)}, u32[]{:S(2)}, u32[]{:S(2)}) collective-permute-start(bf16[16,8,64,512]{3,2,1,0:T(8,128)(2,1)} %get-tuple-element.83), channel_id=1, source_target_pairs={{0,1},{1,0},{2,3},{3,2},{4,5},{5,4},{6,7},{7,6},{8,9},{9,8},{10,11... | collective-permute-start | bytes 25165832 | tf_op jit(solution)/shard_map/ppermute | solution.py:404
  198.7 68.6 %collective-permute-start.9 = (bf16[2,2,512,512]{3,2,0,1:T(8,128)(2,1)}, bf16[2,2,512,512]{3,2,0,1:T(8,128)(2,1)S(1)}, u32[]{:S(2)}, u32[]{:S(2)}) collective-permute-start(bf16[2,2,512,512]{3,2,0,1:T(8,128)(2,1)} %fusion), channel_id=1, source_target_pairs={{0,2},{2,0},{1,3},{3,1},{4,6},{6,4},{5,7},{7,5},{8,10},{10,8},{9,1... | collective-permute-start | bytes 6291464 | tf_op jit(solution)/shard_map/ppermute | solution.py:404
  202.8 64.4 %collective-permute-start.10 = (bf16[2,2,512,512]{3,2,0,1:T(8,128)(2,1)}, bf16[2,2,512,512]{3,2,0,1:T(8,128)(2,1)}, u32[]{:S(2)}, u32[]{:S(2)}) collective-permute-start(bf16[2,2,512,512]{3,2,0,1:T(8,128)(2,1)} %fusion.1), channel_id=1, source_target_pairs={{0,4},{4,0},{1,5},{5,1},{2,6},{6,2},{3,7},{7,3},{8,12},{12,8},{9,1... | collective-permute-start | bytes 6291464 | tf_op jit(solution)/shard_map/ppermute | solution.py:404
  267.1 80.0 %collective-permute-start.14 = (bf16[1024,2048]{1,0:T(8,128)(2,1)}, bf16[1024,2048]{1,0:T(8,128)(2,1)}, u32[]{:S(2)}, u32[]{:S(2)}) collective-permute-start(bf16[1024,2048]{1,0:T(8,128)(2,1)} %get-tuple-element.113), channel_id=1, source_target_pairs={{0,1},{1,0},{2,3},{3,2},{4,5},{5,4},{6,7},{7,6},{8,9},{9,8},{10,11... | collective-permute-start | bytes 12582920 | tf_op jit(solution)/shard_map/ppermute | solution.py:404
  271.6 28.0 %collective-permute-start.11 = (bf16[2,512,512]{2,1,0:T(8,128)(2,1)}, bf16[2,512,512]{2,1,0:T(8,128)(2,1)S(1)}, u32[]{:S(2)}, u32[]{:S(2)}) collective-permute-start(bf16[2,512,512]{2,1,0:T(8,128)(2,1)} %get-tuple-element.153), channel_id=1, source_target_pairs={{0,4},{4,0},{1,5},{5,1},{2,6},{6,2},{3,7},{7,3},{8,12},{12,8},{9,1... | collective-permute-start | bytes 3145736 | tf_op jit(solution)/shard_map/ppermute | solution.py:404
  271.7 27.9 %collective-permute-start.12 = (bf16[2,512,512]{2,1,0:T(8,128)(2,1)S(1)}, bf16[2,512,512]{2,1,0:T(8,128)(2,1)S(1)}, u32[]{:S(2)}, u32[]{:S(2)}) collective-permute-start(bf16[2,512,512]{2,1,0:T(8,128)(2,1)S(1)} %get-tuple-element.152), channel_id=1, source_target_pairs={{0,2},{2,0},{1,3},{3,1},{4,6},{6,4},{5,7},{7,5},{8,10},{10,8},{9,1... | collective-permute-start | bytes 3145736 | tf_op jit(solution)/shard_map/ppermute | solution.py:404
  304.1 26.6 %collective-permute-start.13 = (bf16[2,512,512]{2,1,0:T(8,128)(2,1)}, bf16[2,512,512]{2,1,0:T(8,128)(2,1)S(1)}, u32[]{:S(2)}, u32[]{:S(2)}) collective-permute-start(bf16[2,512,512]{2,1,0:T(8,128)(2,1)} %select_convert_fusion), channel_id=1, source_target_pairs={{0,8},{8,0},{16,24},{24,16},{1,9},{9,1},{17,25},{25,17},{2,10},{10... | collective-permute-start | bytes 3145736 | tf_op jit(solution)/shard_map/ppermute | solution.py:404
  342.6 32.4 %collective-permute-start.23 = (bf16[1,512,512]{2,1,0:T(8,128)(2,1)S(1)}, bf16[1,512,512]{2,1,0:T(8,128)(2,1)S(1)}, u32[]{:S(2)}, u32[]{:S(2)}) collective-permute-start(bf16[1,512,512]{2,1,0:T(8,128)(2,1)S(1)} %dynamic-slice_convert_fusion), channel_id=1, source_target_pairs={{0,16},{8,24},{16,0},{24,8},{1,17},{9,25},{17,1},{25,9},{2,18},{10... | collective-permute-start | bytes 1572872 | tf_op jit(solution)/shard_map/ppermute | solution.py:404
  353.9 25.6 %collective-permute-start.16 = (bf16[2,2,64,2048]{3,2,0,1:T(8,128)(2,1)}, bf16[2,2,64,2048]{3,2,0,1:T(8,128)(2,1)}, u32[]{:S(2)}, u32[]{:S(2)}) collective-permute-start(bf16[2,2,64,2048]{3,2,0,1:T(8,128)(2,1)} %fusion.6), channel_id=1, source_target_pairs={{0,2},{2,0},{1,3},{3,1},{4,6},{6,4},{5,7},{7,5},{8,10},{10,8},{9,1... | collective-permute-start | bytes 3145736 | tf_op jit(solution)/shard_map/ppermute | solution.py:404
  356.7 25.3 %collective-permute-start.17 = (bf16[2,2,64,2048]{3,2,0,1:T(8,128)(2,1)}, bf16[2,2,64,2048]{3,2,0,1:T(8,128)(2,1)}, u32[]{:S(2)}, u32[]{:S(2)}) collective-permute-start(bf16[2,2,64,2048]{3,2,0,1:T(8,128)(2,1)} %fusion.7), channel_id=1, source_target_pairs={{0,4},{4,0},{1,5},{5,1},{2,6},{6,2},{3,7},{7,3},{8,12},{12,8},{9,1... | collective-permute-start | bytes 3145736 | tf_op jit(solution)/shard_map/ppermute | solution.py:404
  377.5 41.4 %collective-permute-start.24 = (f32[256,512]{1,0:T(8,128)}, f32[256,512]{1,0:T(8,128)}, u32[]{:S(2)}, u32[]{:S(2)}) collective-permute-start(f32[256,512]{1,0:T(8,128)} %constant_dynamic-slice_fusion.4), channel_id=1, source_target_pairs={{0,1},{1,0},{2,3},{3,2},{4,5},{5,4},{6,7},{7,6},{8,9},{9,8},{10,11... | collective-permute-start | bytes 1572872 | tf_op jit(solution)/shard_map/ppermute | solution.py:404
  385.1 29.5 %collective-permute-start.18 = (bf16[2,64,2048]{2,1,0:T(8,128)(2,1)}, bf16[2,64,2048]{2,1,0:T(8,128)(2,1)S(1)}, u32[]{:S(2)}, u32[]{:S(2)}) collective-permute-start(bf16[2,64,2048]{2,1,0:T(8,128)(2,1)} %get-tuple-element.155), channel_id=1, source_target_pairs={{0,4},{4,0},{1,5},{5,1},{2,6},{6,2},{3,7},{7,3},{8,12},{12,8},{9,1... | collective-permute-start | bytes 1572872 | tf_op jit(solution)/shard_map/ppermute | solution.py:404
  385.4 29.2 %collective-permute-start.19 = (bf16[2,64,2048]{2,1,0:T(8,128)(2,1)}, bf16[2,64,2048]{2,1,0:T(8,128)(2,1)}, u32[]{:S(2)}, u32[]{:S(2)}) collective-permute-start(bf16[2,64,2048]{2,1,0:T(8,128)(2,1)} %get-tuple-element.154), channel_id=1, source_target_pairs={{0,2},{2,0},{1,3},{3,1},{4,6},{6,4},{5,7},{7,5},{8,10},{10,8},{9,1... | collective-permute-start | bytes 1572872 | tf_op jit(solution)/shard_map/ppermute | solution.py:404
  416.9 14.4 %collective-permute-start.20 = (bf16[2,64,2048]{2,1,0:T(8,128)(2,1)S(1)}, bf16[2,64,2048]{2,1,0:T(8,128)(2,1)S(1)}, u32[]{:S(2)}, u32[]{:S(2)}) collective-permute-start(bf16[2,64,2048]{2,1,0:T(8,128)(2,1)S(1)} %select_convert_fusion.1), channel_id=1, source_target_pairs={{0,8},{8,0},{16,24},{24,16},{1,9},{9,1},{17,25},{25,17},{2,10},{10... | collective-permute-start | bytes 1572872 | tf_op jit(solution)/shard_map/ppermute | solution.py:404
  422.0 15.0 %collective-permute-start.27 = (f32[104,128]{1,0:T(8,128)S(1)}, f32[104,128]{1,0:T(8,128)S(1)}, u32[]{:S(2)}, u32[]{:S(2)}) collective-permute-start(f32[104,128]{1,0:T(8,128)S(1)} %fusion.30), channel_id=1, source_target_pairs={{0,4},{4,0},{1,5},{5,1},{2,6},{6,2},{3,7},{7,3},{8,12},{12,8},{9,1... | collective-permute-start | bytes 159752 | tf_op jit(solution)/shard_map/ppermute | solution.py:404
  433.8 16.0 %collective-permute-start.21 = (bf16[1,64,2048]{2,1,0:T(8,128)(2,1)S(1)}, bf16[1,64,2048]{2,1,0:T(8,128)(2,1)S(1)}, u32[]{:S(2)}, u32[]{:S(2)}) collective-permute-start(bf16[1,64,2048]{2,1,0:T(8,128)(2,1)S(1)} %dynamic-slice_convert_fusion.1), channel_id=1, source_target_pairs={{0,16},{8,24},{16,0},{24,8},{1,17},{9,25},{17,1},{25,9},{2,18},{10... | collective-permute-start | bytes 786440 | tf_op jit(solution)/shard_map/ppermute | solution.py:404
  (42 other events, 333.6 us)
Sparse Core Ops, SparseCore 0:
  11.5 107.0 all-gather.2
  122.0 74.9 all-gather.4

commit v3 on v2

--- a/solution.py
+++ b/solution.py
@@ -336,8 +336,26 @@
     )(core, *args, *after)[0]
 
 
+def grad_normed_kernel(core, grad_hidden, w_in, grad_nm):
+    grad_nm[...] = mul(grad_hidden[...], w_in[...], 1, 1)
+
+
+def grads_normed(core, grad_hidden, w_in):
+    length = grad_hidden.shape[0]
+    return call(
+        grad_normed_kernel, (length // TOKEN_TILE,),
+        [
+            pl.BlockSpec((TOKEN_TILE, FF), lambda g, core: (g, 0)),
+            pl.BlockSpec((D, FF), lambda g, core: (0, 0), pipeline_mode=pl.Buffered(1)),
+        ],
+        [pl.BlockSpec((TOKEN_TILE, D), lambda g, core: (g, 0))],
+        [jax.ShapeDtypeStruct((length, D), f32)], (grad_hidden, w_in),
+        flops=9 * 10**9, moved=2 * 10**7,
+    )(core, grad_hidden, w_in)[0]
+
+
 def input_kernel(
-    core, tokens, cot, gq, gk, gv, grad_hidden, w_qkv, w_in, gain_one, gain_two, input_grad, sums
+    core, tokens, cot, gq, gk, gv, grad_nm, w_qkv, gain_one, gain_two, input_grad, sums
 ):
     inputs = tokens[...].astype(f32)
     centre = inputs - jnp.mean(inputs, axis=-1, keepdims=True)
@@ -346,7 +364,7 @@
     normed = centre * rstd
     joined = jnp.concatenate([gq[...], gk[...], gv[...]], axis=0)
     grad_na = mul(joined, w_qkv[...], 0, 1)
-    grad_nm = mul(grad_hidden[...], w_in[...], 1, 1)
+    grad_nm = grad_nm[...]
     grad_normed = grad_na * gain_one[...] + grad_nm * gain_two[...]
     cotangent = cot[...].astype(f32)
     input_grad[...] = cotangent + rstd * (
@@ -363,17 +381,16 @@
         sums[at : at + 1, :] += jnp.sum(terms, axis=0, keepdims=True)
 
 
-def input_grads(core, tokens, cot, joined, grad_hidden, weights, w_in, gains, after):
+def input_grads(core, tokens, cot, joined, grad_nm, weights, gains, after):
     length = tokens.shape[0]
     tile = pl.BlockSpec((TOKEN_TILE, D), lambda g, core: (g, 0))
     turned = pl.BlockSpec((D, TOKEN_TILE), lambda g, core: (0, g))
     once = functools.partial(pl.BlockSpec, pipeline_mode=pl.Buffered(1))
-    args = (tokens, cot) + joined + (grad_hidden, weights, w_in) + gains
+    args = (tokens, cot) + joined + (grad_nm, weights) + gains
     sd = jax.ShapeDtypeStruct
     return call(
         input_kernel, (length // TOKEN_TILE,),
-        [tile, tile] + [turned] * 3 + [pl.BlockSpec((TOKEN_TILE, FF), lambda g, core: (g, 0))]
-        + [once((D, 3 * D), lambda g, core: (0, 0)), once((D, FF), lambda g, core: (0, 0))]
+        [tile, tile] + [turned] * 3 + [tile, once((D, 3 * D), lambda g, core: (0, 0))]
         + [whole_block((1, D))] * 2,
         [tile, whole_block((8, D))],
         [sd((length, D), f32), sd((8, D), f32)], args, after, flops=15 * 10**9, moved=4 * 10**7,
@@ -572,37 +589,41 @@
     )
     far, near = grads_in(core_ref, nm_t, grad_hidden, far, near)
     deep = 2 * FF // blocks
+    grad_nm = grads_normed(core_ref, later(grad_hidden, far), w_in_all)
+    came_hidden = later(links.swap("c", far), grad_nm)
     hidden = Scatter(
-        links, near.reshape(blocks * deep, HALF), links.swap("c", far).reshape(blocks * deep, HALF)
+        links, near.reshape(blocks * deep, HALF), came_hidden.reshape(blocks * deep, HALF)
     )
     heads = functools.partial(attention, core_ref)
 
     def common(*after):
-        return (later(start, *after), cos, sin, na_t, cotangent, weights, bias_qkv)
-
-    far, *kept = heads(False, 0, 2, *common(*hidden.first))
+        first = later(start, *after) if after else start
+        return (first, cos, sin, na_t, cotangent, weights, bias_qkv)
+
+    far, *kept = heads(False, 0, 1, *common(*hidden.first))
+    far, *kept = heads(False, 1, 1, *common(), kept, far)
     came_heads = links.swap("c", far)
     hidden.step_one(kept[4])
     near, *kept = heads(True, 0, 1, *common(*hidden.second), kept)
     hidden.step_two(kept[4])
     near, *kept = heads(True, 1, 1, *common(hidden.send), kept, near)
     merged, *joined = kept[:4]
-    hidden.advance(kept[4])
-    out_far, near = grads_out(core_ref, merged, later(cotangent, hidden.send), near)
+    out_far, near = grads_out(core_ref, merged, cotangent, near)
     came_out = links.swap("c", out_far)
     last = Scatter(
         links, near, lax.dynamic_update_slice(came_heads, came_out, (0, 3 * HALF))
     )
     output = outputs(
-        core_ref, later(tokens, *last.first, hidden.send), merged, active, weights, wd_near, wd_far,
+        core_ref, later(tokens, *last.first), merged, active, weights, wd_near, wd_far,
         (b_out + b_down).reshape(1, D), (),
     )
     last.step_one(output)
+    hidden.advance(output)
     input_grad, sums = input_grads(
-        core_ref, later(tokens, *last.second), cotangent, tuple(joined), grad_hidden, weights, w_in_all,
-        gains, (output,),
-    )
-    hidden.advance(output)
+        core_ref, later(tokens, *last.second, hidden.send), cotangent, tuple(joined), grad_nm, weights, gains,
+        (output,),
+    )
+    hidden.advance(sums)
     held = hidden.finish()
     deep = deep // 2
     held = jnp.concatenate(
@@ -619,7 +640,7 @@
     vector_terms = jnp.concatenate(
         [part[:, 0] for part in kept[4:]] + [sums[0], sum_in[0], sums[0], sums[1], sums[2], sums[3], sums[4]]
     )
-    vector_total = links.total(vector_terms.reshape(-1, 128)).reshape(-1)
+    vector_total = links.total(later(vector_terms, last.send).reshape(-1, 128)).reshape(-1)
     count_own = vectors.shape[0]
     grad_vectors = lax.dynamic_slice_in_dim(
         vector_total, lax.axis_index(every) * count_own, count_own

time: 493 us -> 483 us (0.980); the launches traced: 490 us -> 473 us
  waiting for transfers between devices: 125 us -> 111 us
  Pallas kernels: 227 us -> 221 us
    pallas_call x0 -> x1, Pallas kernels: none -> 14.9 us  [grads_normed(): call(grad_normed_kernel, (length // TOKEN_TILE,), [pl.BlockSpec((TOKEN_TI...]
    ppermute x35, waiting for transfers between devices: 119 us -> 105 us  [swap(): lax.ppermute(value, axis, [(i, i ^ bit) for i in range(self.sizes[axis])])]
    pallas_call x1, Pallas kernels: 27.5 us -> 16.4 us  [input_grads(): call(input_kernel, (length // TOKEN_TILE,), [tile, tile] + [turned] * 3 +...]
    pallas_call x3 -> x4, Pallas kernels: 115 us -> 105 us  [attention(): call(attention_kernel, (parts,), in_specs, out_specs, out_shape, args, ke...]
  transfers between devices with their start and end apart: 37 -> 37, of which waited for: 20 -> 20; matrix products, arithmetic and copies ran while one was open for 14% -> 15% of each run, Pallas kernels for 46% -> 47%
where the time goes in v3:
time: 483 us; the launch traced here: 473 us
  Pallas kernels  221 us (46%)
  waiting for transfers between devices  111 us (23%)
  other arithmetic  61.6 us (13%)
  starting transfers between devices  37.1 us (8%)
  local copies, waits for them, and re-layouts  21.4 us (4%)
  between operations  20.5 us (4%)
    ppermute x35, waiting for transfers between devices, swap(): lax.ppermute(value, axis, [(i, i ^ bit) for i in range(self.sizes[axis])])  105 us
    pallas_call x4, Pallas kernels, attention(): call(attention_kernel, (parts,), in_specs, out_specs, out_shape, args, ke...  105 us
    pallas_call x1, Pallas kernels, ffn(): call(ffn_kernel, (FF // FF_TILE,), [whole_block((length, D))] * 2 + [colu...  38.3 us
    ppermute x35, starting transfers between devices, swap(): lax.ppermute(value, axis, [(i, i ^ bit) for i in range(self.sizes[axis])])  37.1 us
    pallas_call x1, Pallas kernels, outputs(): call(output_kernel, (length // TOKEN_TILE,), [tile, turned, pl.BlockSpec(...  18 us
    pallas_call x1, Pallas kernels, input_grads(): call(input_kernel, (length // TOKEN_TILE,), [tile, tile] + [turned] * 3 +...  16.4 us
    pallas_call x1, Pallas kernels, grads_normed(): call(grad_normed_kernel, (length // TOKEN_TILE,), [pl.BlockSpec((TOKEN_TI...  14.9 us
    pallas_call x1, Pallas kernels, grads_in(): call(grad_in_kernel, (2 * half,), [whole_block((D, length)), pl.BlockSpec...  14.6 us
  transfers between devices with their start and end apart: 37, of which 20 were waited for; matrix products, arithmetic and copies ran while one was open for 15% of the time, Pallas kernels for 47%

profile of v3, /device:TPU:0, one launch (start us, length us, event | category | flops | bytes accessed | tf_op | source)
XLA Modules:
  0.0 473.1 jit_solution(12765739717763704541)
XLA Ops:
  13.3 4.0 collective-permute-start.1
  17.4 16.1 %collective-permute-done.1 = bf16[1,256,512]{2,1,0:T(8,128)(2,1)S(1)} collective-permute-done((bf16[1,256,512]{2,1,0:T(8,128)(2,1)S(1)}, bf16[1,256,512]{2,1,0:T(8,128)(2,1)S(1)}, u32[]{:S(2)}, u32[]{:S(2)}) %collective-permute-start.1) | collective-permute-done | bytes 262176 | tf_op jit(solution)/shard_map/ppermute | solution.py:421
  35.9 17.5 %collective-permute-done.2.refs_2_ = bf16[2,256,512]{2,1,0:T(8,128)(2,1)S(1)} collective-permute-done((bf16[2,256,512]{2,1,0:T(8,128)(2,1)S(1)}, bf16[2,256,512]{2,1,0:T(8,128)(2,1)S(1)}, u32[]{:S(2)}, u32[]{:S(2)}) %collective-permute-start.2) | collective-permute-done | bytes 524320 | tf_op jit(solution)/shard_map/ppermute | solution.py:421
  56.7 8.3 %collective-permute-done.3 = bf16[2,1,1,1,256,512]{5,4,0,3,2,1:T(8,128)(2,1)S(1)} collective-permute-done((bf16[2,1,1,1,256,512]{5,4,0,3,2,1:T(8,128)(2,1)S(1)}, bf16[2,1,1,1,256,512]{5,4,0,3,2,1:T(8,128)(2,1)S(1)}, u32[]{:S(2)}, u32[]{:S(2)}) %collective-permute-start.3) | collective-permute-done | bytes 524320 | tf_op jit(solution)/shard_map/ppermute | solution.py:421
  74.0 30.1 %collective-permute-done.4 = bf16[2,1,2,1,256,512]{5,4,0,3,2,1:T(8,128)(2,1)} collective-permute-done((bf16[2,1,2,1,256,512]{5,4,0,3,2,1:T(8,128)(2,1)}, bf16[2,1,2,1,256,512]{5,4,0,3,2,1:T(8,128)(2,1)}, u32[]{:S(2)}, u32[]{:S(2)}) %collective-permute-start.4) | collective-permute-done | bytes 1048608 | tf_op jit(solution)/shard_map/ppermute | solution.py:421
  112.7 5.9 %all-gather.3.cloned.1.call-done.refs_3_.refs_2_ = bf16[1024,4224]{1,0:T(8,128)(2,1)} async-done(((bf16[32,4224]{1,0:T(8,128)(2,1)}), bf16[1024,4224]{1,0:T(8,128)(2,1)}) %all-gather.3.cloned.1.call-update) | async-done | bytes 8650768 | tf_op jit(solution)/shard_map/all_gather | solution.py:559
  121.2 6.0 %norm_kernel.1 = (bf16[1024,1024]{1,0:T(8,128)(2,1)}, bf16[1024,1024]{1,0:T(8,128)(2,1)}, bf16[1024,1024]{1,0:T(8,128)(2,1)}, bf16[1024,1024]{1,0:T(8,128)(2,1)}) custom-call(s32[1]{0:T(128)} %bitcast.refs_0_, bf16[1024,1024]{1,0:T(8,128)(2,1)} %refs_1_.3, f32[1,1024]{1,0:T(1,128)} %bitcast.218, f32[1,1024]{1,0:T(1,128)} %bitcast.221, f32[1,1024]{1,0:T(1,128)} %bitcast.216, ...), custom_call_target="tpu_custom_call" | custom-call | flops 10000000 | bytes 10000000 | tf_op jit(solution)/shard_map/norm_kernel/pallas_call | solution.py:116
  127.1 38.3 %ffn_kernel.1 = (bf16[16,512,512]{2,1,0:T(8,128)(2,1)}, bf16[16,512,512]{2,1,0:T(8,128)(2,1)}, bf16[1024,4096]{1,0:T(8,128)(2,1)}, bf16[1024,4096]{1,0:T(8,128)(2,1)}, f32[1,4096]{1,0:T(1,128)}) custom-call(s32[1]{0:T(128)} %bitcast.refs_0_, bf16[1024,1024]{1,0:T(8,128)(2,1)} %get-tuple-element.88.refs_1_, bf16[1024,1024]{1,0:T(8,128)(2,1)} %refs_2_.5, ...), custom_call_target="tpu_custom_call" | custom-call | flops 30000001024 | bytes 50000000 | tf_op jit(solution)/shard_map/ffn_kernel/pallas_call | solution.py:271
  165.4 14.6 %grad_in_kernel.1 = (bf16[16,8,64,512]{3,2,1,0:T(8,128)(2,1)}, bf16[16,8,64,512]{3,2,1,0:T(8,128)(2,1)}) custom-call(s32[1]{0:T(128)} %bitcast.refs_0_, bf16[1024,1024]{1,0:T(8,128)(2,1)} %get-tuple-element.87.refs_1_, bf16[1024,4096]{1,0:T(8,128)(2,1)} %get-tuple-element.94.refs_2_.refs_1_, ...), custom_call_target="tpu_custom_call", output_to_operand_aliasing={{0}: (3, {}), {1}: (4, {})} | custom-call | flops 8999999488 | bytes 20000000 | tf_op jit(solution)/shard_map/grad_in_kernel/pallas_call | solution.py:299
  184.1 14.9 %grad_normed_kernel.1.refs_6_ = f32[1024,1024]{1,0:T(8,128)} custom-call(s32[1]{0:T(128)} %bitcast.refs_0_, bf16[1024,4096]{1,0:T(8,128)(2,1)} %get-tuple-element.94.refs_2_.refs_1_, bf16[1024,4224]{1,0:T(8,128)(2,1)} %all-gather.3.cloned.1.call-done.refs_3_.refs_2_), custom_call_target="tpu_custom_call" | custom-call | flops 8999999488 | bytes 20000000 | tf_op jit(solution)/shard_map/grad_normed_kernel/pallas_call | solution.py:345
  199.0 4.2 fusion
  204.1 4.2 fusion.1
  209.8 26.3 %attention_kernel.4 = (bf16[1024,2048]{1,0:T(8,128)(2,1)}, bf16[1024,1024]{1,0:T(8,128)(2,1)}, bf16[1024,1024]{1,0:T(8,128)(2,1)}, bf16[1024,1024]{1,0:T(8,128)(...) custom-call(s32[1]{0:T(128)} %bitcast.refs_0_, ...), custom_call_target="tpu_custom_call" | custom-call | flops 24999999488 | bytes 20000000 | tf_op jit(solution)/shard_map/attention_kernel/pallas_call | solution.py:207
  236.1 26.3 %attention_kernel.5 = (bf16[1024,2048]{1,0:T(8,128)(2,1)}, bf16[1024,1024]{1,0:T(8,128)(2,1)}, bf16[1024,1024]{1,0:T(8,128)(2,1)}, bf16[1024,1024]{1,0:T(8,128)(...) custom-call(s32[1]{0:T(128)} %bitcast.refs_0_, ...), custom_call_target="tpu_custom_call", output_to_operand_aliasing={{0}: (13, {}), {1}: (14, {}), {2}: (15, {}), {3}: (16, {}),... | custom-call | flops 24999999488 | bytes 20000000 | tf_op jit(solution)/shard_map/attention_kernel/pallas_call | solution.py:207
  262.4 5.1 %fusion.3 = (bf16[2,512,512]{2,1,0:T(8,128)(2,1)S(1)}, bf16[2,512,512]{2,1,0:T(8,128)(2,1)}) fusion(bf16[2,2,512,512]{3,2,0,1:T(8,128)(2,1)} %collective-permute-done.10, s32[]{:T(128)S(6)} %select_n.253, bf16[2,2,2,2,512,512]{5,4,3,2,1,0:T(8,128)(2,1)} %bitcast.17, s32[]{:T(128)S(6)} %select_n.257, bf16[2,2,2,2,512,512]{5,4,3,2,1,0:T(8,128)(2,1)} %bitcast.191, ...), kind=kLoop, calls=%fused_computation.7 | loop fusion | flops 6291456 | bytes 8388624 | tf_op jit(solution)/shard_map/convert_element_type | solution.py:501
  269.2 26.3 %attention_kernel.6 = (bf16[1024,2048]{1,0:T(8,128)(2,1)}, bf16[1024,1024]{1,0:T(8,128)(2,1)}, bf16[1024,1024]{1,0:T(8,128)(2,1)}, bf16[1024,1024]{1,0:T(8,128)(...) custom-call(s32[1]{0:T(128)} %bitcast.refs_0_, ...), custom_call_target="tpu_custom_call", output_to_operand_aliasing={{1}: (13, {}), {2}: (14, {}), {3}: (15, {}), {4}: (16, {}),... | custom-call | flops 24999999488 | bytes 20000000 | tf_op jit(solution)/shard_map/attention_kernel/pallas_call | solution.py:207
  295.6 4.9 %select_convert_fusion = bf16[2,512,512]{2,1,0:T(8,128)(2,1)} fusion(pred[]{:T(512)S(6)} %eq.30, bf16[2,512,512]{2,1,0:T(8,128)(2,1)S(1)} %collective-permute-done.12, bf16[2,2,512,512]{3,2,0,1:T(8,128)(2,1)} %collective-permute-done.10, s32[]{:T(128)S(6)} %select_n.252, bf16[2,2,2,2,512,512]{5,4,3,2,1,0:T(8,128)(2,1)} %bitcast.17, s32[]{:T(128)S(6)} %select_n.257, ...), kind=kLoop, calls=%fused_computation.15 | loop fusion | flops 8388608 | bytes 9437193 | tf_op jit(solution)/shard_map/convert_element_type | solution.py:511
  300.5 26.3 %attention_kernel.7 = (bf16[1024,2048]{1,0:T(8,128)(2,1)}, bf16[1024,1024]{1,0:T(8,128)(2,1)}, bf16[1024,1024]{1,0:T(8,128)(2,1)}, bf16[1024,1024]{1,0:T(8,128)(...) custom-call(s32[1]{0:T(128)} %bitcast.refs_0_, ...), custom_call_target="tpu_custom_call", output_to_operand_aliasing={{0}: (13, {}), {1}: (14, {}), {2}: (15, {}), {3}: (16, {}),... | custom-call | flops 24999999488 | bytes 20000000 | tf_op jit(solution)/shard_map/attention_kernel/pallas_call | solution.py:207
  326.8 6.1 %grad_out_kernel.1 = (bf16[1024,512]{1,0:T(8,128)(2,1)}, bf16[1024,2048]{1,0:T(8,128)(2,1)}) custom-call(s32[1]{0:T(128)} %bitcast.refs_0_, bf16[1024,1024]{1,0:T(8,128)(2,1)} %get-tuple-element.127.refs_1_.refs_2_, bf16[1024,1024]{1,0:T(8,128)(2,1)} %refs_2_.5, bf16[1024,2048]{1,0:T(8,128)(2,1)} %get-tuple-element.128.refs_3_), custom_call_target="tpu_custom_call", output_to_operand_aliasing={{1}: (3, {})} | custom-call | flops 3000000000 | bytes 10000000 | tf_op jit(solution)/shard_map/grad_out_kernel/pallas_call | solution.py:233
  346.2 18.0 %output_kernel.1.refs_10_ = bf16[1024,1024]{1,0:T(8,128)(2,1)} custom-call(s32[1]{0:T(128)} %bitcast.refs_0_, bf16[1024,1024]{1,0:T(8,128)(2,1)} %refs_1_.3, bf16[1024,1024]{1,0:T(8,128)(2,1)} %get-tuple-element.127.refs_1_.refs_2_, bf16[1024,4096]{1,0:T(8,128)(2,1)} %get-tuple-element.133.refs_3_, ...), custom_call_target="tpu_custom_call" | custom-call | flops 11000000512 | bytes 30000000 | tf_op jit(solution)/shard_map/output_kernel/pallas_call | solution.py:330
  364.2 4.6 convert_add_fusion.4
  377.2 16.4 %input_kernel.1 = (f32[1024,1024]{1,0:T(8,128)}, f32[8,1024]{1,0:T(8,128)}) custom-call(s32[1]{0:T(128)} %bitcast.refs_0_, bf16[1024,1024]{1,0:T(8,128)(2,1)} %refs_1_.3, bf16[1024,1024]{1,0:T(8,128)(2,1)} %refs_2_.5, bf16[1024,1024]{1,0:T(8,128)(2,1)} %get-tuple-element.138.refs_3_, bf16[1024,1024]{1,0:T(8,128)(2,1)} %get-tuple-element.139.refs_4_, ...), custom_call_target="tpu_custom_call" | custom-call | flops 15000000512 | bytes 40000000 | tf_op jit(solution)/shard_map/input_kernel/pallas_call | solution.py:391
  407.1 8.0 %collective-permute-done.20 = bf16[2,64,2048]{2,1,0:T(8,128)(2,1)S(1)} collective-permute-done((bf16[2,64,2048]{2,1,0:T(8,128)(2,1)}, bf16[2,64,2048]{2,1,0:T(8,128)(2,1)S(1)}, u32[]{:S(2)}, u32[]{:S(2)}) %collective-permute-start.20) | collective-permute-done | bytes 524320 | tf_op jit(solution)/shard_map/ppermute | solution.py:421
  428.6 5.0 %collective-permute-done.21 = bf16[1,64,2048]{2,1,0:T(8,128)(2,1)S(1)} collective-permute-done((bf16[1,64,2048]{2,1,0:T(8,128)(2,1)S(1)}, bf16[1,64,2048]{2,1,0:T(8,128)(2,1)S(1)}, u32[]{:S(2)}, u32[]{:S(2)}) %collective-permute-start.21) | collective-permute-done | bytes 262176 | tf_op jit(solution)/shard_map/ppermute | solution.py:421
  (233 shorter events, 115.1 us)
Async XLA Ops:
  7.2 111.4 %all-gather.3.cloned.1.call-start = ((), (), s32[]{:S(2)}) async-start(), calls=%async_computation | async-start | bytes 8921088 | tf_op jit(solution)/shard_map/all_gather | solution.py:559
  9.9 199.9 %all-gather.5.cloned.1.call-start = ((), (), s32[]{:S(2)}) async-start(), calls=%async_computation.1 | async-start | bytes 8650752 | tf_op jit(solution)/shard_map/all_gather | solution.py:569
  13.3 20.1 %collective-permute-start.1 = (bf16[1,256,512]{2,1,0:T(8,128)(2,1)S(1)}, bf16[1,256,512]{2,1,0:T(8,128)(2,1)S(1)}, u32[]{:S(2)}, u32[]{:S(2)}) collective-permute-start(bf16[1,256,512]{2,1,0:T(8,128)(2,1)S(1)} %maximum_select_fusion.3), channel_id=1, source_target_pairs={{0,16},{8,24},{16,0},{24,8},{1,17},{9,25},{17,1},{25,9},{2,18},{10... | collective-permute-start | bytes 786440 | tf_op jit(solution)/shard_map/ppermute | solution.py:421
  33.5 19.9 %collective-permute-start.2 = (bf16[2,256,512]{2,1,0:T(8,128)(2,1)S(1)}, bf16[2,256,512]{2,1,0:T(8,128)(2,1)S(1)}, u32[]{:S(2)}, u32[]{:S(2)}) collective-permute-start(bf16[2,256,512]{2,1,0:T(8,128)(2,1)S(1)} %maximum_select_fusion.2), channel_id=1, source_target_pairs={{0,8},{8,0},{16,24},{24,16},{1,9},{9,1},{17,25},{25,17},{2,10},{10... | collective-permute-start | bytes 1572872 | tf_op jit(solution)/shard_map/ppermute | solution.py:421
  53.5 11.5 %collective-permute-start.3 = (bf16[2,1,1,1,256,512]{5,4,0,3,2,1:T(8,128)(2,1)S(1)}, bf16[2,1,1,1,256,512]{5,4,0,3,2,1:T(8,128)(2,1)S(1)}, u32[]{:S(2)}, u32[]{:S(2)}) collective-permute-start(bf16[2,1,1,1,256,512]{5,4,0,3,2,1:T(8,128)(2,1)S(1)} %get-tuple-element.182), channel_id=1, source_target_pairs={{0,4},{4,0},{1,5},{5,1},{2,6},{6,2},{3,7},{7,3},{8,12},{12,8},{9,1... | collective-permute-start | bytes 1572872 | tf_op jit(solution)/shard_map/ppermute | solution.py:421
  55.0 12.5 %collective-permute-start.5 = (bf16[2,1,1,1,256,512]{5,4,0,3,2,1:T(8,128)(2,1)S(1)}, bf16[2,1,1,1,256,512]{5,4,0,3,2,1:T(8,128)(2,1)S(1)}, u32[]{:S(2)}, u32[]{:S(2)}) collective-permute-start(bf16[2,1,1,1,256,512]{5,4,0,3,2,1:T(8,128)(2,1)S(1)} %get-tuple-element.181), channel_id=1, source_target_pairs={{0,2},{2,0},{1,3},{3,1},{4,6},{6,4},{5,7},{7,5},{8,10},{10,8},{9,1... | collective-permute-start | bytes 1572872 | tf_op jit(solution)/shard_map/ppermute | solution.py:421
  66.2 37.9 %collective-permute-start.4 = (bf16[2,1,2,1,256,512]{5,4,0,3,2,1:T(8,128)(2,1)}, bf16[2,1,2,1,256,512]{5,4,0,3,2,1:T(8,128)(2,1)}, u32[]{:S(2)}, u32[]{:S(2)}) collective-permute-start(bf16[2,1,2,1,256,512]{5,4,0,3,2,1:T(8,128)(2,1)} %maximum_select_fusion), channel_id=1, source_target_pairs={{0,2},{2,0},{1,3},{3,1},{4,6},{6,4},{5,7},{7,5},{8,10},{10,8},{9,1... | collective-permute-start | bytes 3145736 | tf_op jit(solution)/shard_map/ppermute | solution.py:421
  68.6 39.0 %collective-permute-start.6 = (bf16[2,1,1,2,256,512]{5,4,0,3,2,1:T(8,128)(2,1)}, bf16[2,1,1,2,256,512]{5,4,0,3,2,1:T(8,128)(2,1)}, u32[]{:S(2)}, u32[]{:S(2)}) collective-permute-start(bf16[2,1,1,2,256,512]{5,4,0,3,2,1:T(8,128)(2,1)} %maximum_select_fusion.1), channel_id=1, source_target_pairs={{0,4},{4,0},{1,5},{5,1},{2,6},{6,2},{3,7},{7,3},{8,12},{12,8},{9,1... | collective-permute-start | bytes 3145736 | tf_op jit(solution)/shard_map/ppermute | solution.py:421
  110.0 17.1 %collective-permute-start.7 = (bf16[4096,512]{1,0:T(8,128)(2,1)}, bf16[4096,512]{1,0:T(8,128)(2,1)}, u32[]{:S(2)}, u32[]{:S(2)}) collective-permute-start(bf16[4096,512]{1,0:T(8,128)(2,1)} %bitcast.12.refs_4_.refs_5_), channel_id=1, source_target_pairs={{0,1},{1,0},{2,3},{3,2},{4,5},{5,4},{6,7},{7,6},{8,9},{9,8},{10,11... | collective-permute-start | bytes 12582920 | tf_op jit(solution)/shard_map/ppermute | solution.py:421
  180.0 19.0 %collective-permute-start.8 = (bf16[16,8,64,512]{3,2,1,0:T(8,128)(2,1)}, bf16[16,8,64,512]{3,2,1,0:T(8,128)(2,1)}, u32[]{:S(2)}, u32[]{:S(2)}) collective-permute-start(bf16[16,8,64,512]{3,2,1,0:T(8,128)(2,1)} %get-tuple-element.93), channel_id=1, source_target_pairs={{0,1},{1,0},{2,3},{3,2},{4,5},{5,4},{6,7},{7,6},{8,9},{9,8},{10,11... | collective-permute-start | bytes 25165832 | tf_op jit(solution)/shard_map/ppermute | solution.py:421
  203.3 59.1 %collective-permute-start.9 = (bf16[2,2,512,512]{3,2,0,1:T(8,128)(2,1)}, bf16[2,2,512,512]{3,2,0,1:T(8,128)(2,1)S(1)}, u32[]{:S(2)}, u32[]{:S(2)}) collective-permute-start(bf16[2,2,512,512]{3,2,0,1:T(8,128)(2,1)} %fusion), channel_id=1, source_target_pairs={{0,2},{2,0},{1,3},{3,1},{4,6},{6,4},{5,7},{7,5},{8,10},{10,8},{9,1... | collective-permute-start | bytes 6291464 | tf_op jit(solution)/shard_map/ppermute | solution.py:421
  208.2 54.2 %collective-permute-start.10 = (bf16[2,2,512,512]{3,2,0,1:T(8,128)(2,1)}, bf16[2,2,512,512]{3,2,0,1:T(8,128)(2,1)}, u32[]{:S(2)}, u32[]{:S(2)}) collective-permute-start(bf16[2,2,512,512]{3,2,0,1:T(8,128)(2,1)} %fusion.1), channel_id=1, source_target_pairs={{0,4},{4,0},{1,5},{5,1},{2,6},{6,2},{3,7},{7,3},{8,12},{12,8},{9,1... | collective-permute-start | bytes 6291464 | tf_op jit(solution)/shard_map/ppermute | solution.py:421
  262.3 72.7 %collective-permute-start.13 = (bf16[1024,2048]{1,0:T(8,128)(2,1)}, bf16[1024,2048]{1,0:T(8,128)(2,1)}, u32[]{:S(2)}, u32[]{:S(2)}) collective-permute-start(bf16[1024,2048]{1,0:T(8,128)(2,1)} %get-tuple-element.130), channel_id=1, source_target_pairs={{0,1},{1,0},{2,3},{3,2},{4,5},{5,4},{6,7},{7,6},{8,9},{9,8},{10,11... | collective-permute-start | bytes 12582920 | tf_op jit(solution)/shard_map/ppermute | solution.py:421
  267.5 28.0 %collective-permute-start.11 = (bf16[2,512,512]{2,1,0:T(8,128)(2,1)}, bf16[2,512,512]{2,1,0:T(8,128)(2,1)S(1)}, u32[]{:S(2)}, u32[]{:S(2)}) collective-permute-start(bf16[2,512,512]{2,1,0:T(8,128)(2,1)} %get-tuple-element.173), channel_id=1, source_target_pairs={{0,4},{4,0},{1,5},{5,1},{2,6},{6,2},{3,7},{7,3},{8,12},{12,8},{9,1... | collective-permute-start | bytes 3145736 | tf_op jit(solution)/shard_map/ppermute | solution.py:421
  268.0 27.5 %collective-permute-start.12 = (bf16[2,512,512]{2,1,0:T(8,128)(2,1)S(1)}, bf16[2,512,512]{2,1,0:T(8,128)(2,1)S(1)}, u32[]{:S(2)}, u32[]{:S(2)}) collective-permute-start(bf16[2,512,512]{2,1,0:T(8,128)(2,1)S(1)} %get-tuple-element.172), channel_id=1, source_target_pairs={{0,2},{2,0},{1,3},{3,1},{4,6},{6,4},{5,7},{7,5},{8,10},{10,8},{9,1... | collective-permute-start | bytes 3145736 | tf_op jit(solution)/shard_map/ppermute | solution.py:421
  333.0 31.2 %collective-permute-start.17 = (bf16[2,512,512]{2,1,0:T(8,128)(2,1)}, bf16[2,512,512]{2,1,0:T(8,128)(2,1)}, u32[]{:S(2)}, u32[]{:S(2)}) collective-permute-start(bf16[2,512,512]{2,1,0:T(8,128)(2,1)} %select_convert_fusion), channel_id=1, source_target_pairs={{0,8},{8,0},{16,24},{24,16},{1,9},{9,1},{17,25},{25,17},{2,10},{10... | collective-permute-start | bytes 3145736 | tf_op jit(solution)/shard_map/ppermute | solution.py:421
  342.4 29.5 %collective-permute-start.15 = (bf16[2,2,64,2048]{3,2,0,1:T(8,128)(2,1)}, bf16[2,2,64,2048]{3,2,0,1:T(8,128)(2,1)}, u32[]{:S(2)}, u32[]{:S(2)}) collective-permute-start(bf16[2,2,64,2048]{3,2,0,1:T(8,128)(2,1)} %fusion.6), channel_id=1, source_target_pairs={{0,2},{2,0},{1,3},{3,1},{4,6},{6,4},{5,7},{7,5},{8,10},{10,8},{9,1... | collective-permute-start | bytes 3145736 | tf_op jit(solution)/shard_map/ppermute | solution.py:421
  344.6 27.3 %collective-permute-start.16 = (bf16[2,2,64,2048]{3,2,0,1:T(8,128)(2,1)}, bf16[2,2,64,2048]{3,2,0,1:T(8,128)(2,1)}, u32[]{:S(2)}, u32[]{:S(2)}) collective-permute-start(bf16[2,2,64,2048]{3,2,0,1:T(8,128)(2,1)} %fusion.7), channel_id=1, source_target_pairs={{0,4},{4,0},{1,5},{5,1},{2,6},{6,2},{3,7},{7,3},{8,12},{12,8},{9,1... | collective-permute-start | bytes 3145736 | tf_op jit(solution)/shard_map/ppermute | solution.py:421
  368.9 26.0 %collective-permute-start.23 = (bf16[1,512,512]{2,1,0:T(8,128)(2,1)S(1)}, bf16[1,512,512]{2,1,0:T(8,128)(2,1)S(1)}, u32[]{:S(2)}, u32[]{:S(2)}) collective-permute-start(bf16[1,512,512]{2,1,0:T(8,128)(2,1)S(1)} %dynamic-slice_convert_fusion), channel_id=1, source_target_pairs={{0,16},{8,24},{16,0},{24,8},{1,17},{9,25},{17,1},{25,9},{2,18},{10... | collective-permute-start | bytes 1572872 | tf_op jit(solution)/shard_map/ppermute | solution.py:421
  375.0 22.4 %collective-permute-start.18 = (bf16[2,64,2048]{2,1,0:T(8,128)(2,1)}, bf16[2,64,2048]{2,1,0:T(8,128)(2,1)S(1)}, u32[]{:S(2)}, u32[]{:S(2)}) collective-permute-start(bf16[2,64,2048]{2,1,0:T(8,128)(2,1)} %get-tuple-element.175), channel_id=1, source_target_pairs={{0,4},{4,0},{1,5},{5,1},{2,6},{6,2},{3,7},{7,3},{8,12},{12,8},{9,1... | collective-permute-start | bytes 1572872 | tf_op jit(solution)/shard_map/ppermute | solution.py:421
  375.8 21.6 %collective-permute-start.19 = (bf16[2,64,2048]{2,1,0:T(8,128)(2,1)}, bf16[2,64,2048]{2,1,0:T(8,128)(2,1)}, u32[]{:S(2)}, u32[]{:S(2)}) collective-permute-start(bf16[2,64,2048]{2,1,0:T(8,128)(2,1)} %get-tuple-element.174), channel_id=1, source_target_pairs={{0,2},{2,0},{1,3},{3,1},{4,6},{6,4},{5,7},{7,5},{8,10},{10,8},{9,1... | collective-permute-start | bytes 1572872 | tf_op jit(solution)/shard_map/ppermute | solution.py:421
  401.1 14.1 %collective-permute-start.20 = (bf16[2,64,2048]{2,1,0:T(8,128)(2,1)}, bf16[2,64,2048]{2,1,0:T(8,128)(2,1)S(1)}, u32[]{:S(2)}, u32[]{:S(2)}) collective-permute-start(bf16[2,64,2048]{2,1,0:T(8,128)(2,1)} %select_convert_fusion.1), channel_id=1, source_target_pairs={{0,8},{8,0},{16,24},{24,16},{1,9},{9,1},{17,25},{25,17},{2,10},{10... | collective-permute-start | bytes 1572872 | tf_op jit(solution)/shard_map/ppermute | solution.py:421
  406.2 15.0 %collective-permute-start.27 = (f32[104,128]{1,0:T(8,128)S(1)}, f32[104,128]{1,0:T(8,128)S(1)}, u32[]{:S(2)}, u32[]{:S(2)}) collective-permute-start(f32[104,128]{1,0:T(8,128)S(1)} %fusion.30), channel_id=1, source_target_pairs={{0,4},{4,0},{1,5},{5,1},{2,6},{6,2},{3,7},{7,3},{8,12},{12,8},{9,1... | collective-permute-start | bytes 159752 | tf_op jit(solution)/shard_map/ppermute | solution.py:421
  417.9 15.7 %collective-permute-start.21 = (bf16[1,64,2048]{2,1,0:T(8,128)(2,1)S(1)}, bf16[1,64,2048]{2,1,0:T(8,128)(2,1)S(1)}, u32[]{:S(2)}, u32[]{:S(2)}) collective-permute-start(bf16[1,64,2048]{2,1,0:T(8,128)(2,1)S(1)} %dynamic-slice_convert_fusion.1), channel_id=1, source_target_pairs={{0,16},{8,24},{16,0},{24,8},{1,17},{9,25},{17,1},{25,9},{2,18},{10... | collective-permute-start | bytes 786440 | tf_op jit(solution)/shard_map/ppermute | solution.py:421
  (44 other events, 337.4 us)
Sparse Core Ops, SparseCore 0:
  11.5 107.0 all-gather.2
  122.0 74.9 all-gather.4
